TPU v7x, 32 devices: a whole 2x2x4 slice. The times are simulated.
32 devices in a mesh: dp: 2 (over core), tensor: 16 (over z, y, x).
Axes of the slice: x: 2, y: 2, z: 4, core: 2. Of those that a mesh axis runs over, the one named last changes fastest.
Arguments:
- gate_pre: bfloat16 [1024, 16384], P('dp', 'tensor'), may hold values from -6 to 6
- up_pre: bfloat16 [1024, 16384], P('dp', 'tensor'), may hold values from -6 to 6
- down_weight: bfloat16 [16384, 4096], P('tensor'), may hold values from -0.0625 to 0.0625
- block_mask: int32 [128, 32], P('tensor'), may hold values from 0 to 1, as said below
- out_grad: bfloat16 [1024, 4096], P(('dp', 'tensor')), may hold values from -6 to 6
Outputs:
- layer_out: bfloat16 [1024, 4096], P(('dp', 'tensor'))
- gate_grad: bfloat16 [1024, 16384], P('dp', 'tensor')
- up_grad: bfloat16 [1024, 16384], P('dp', 'tensor')
- weight_grad: bfloat16 [16384, 4096], P('tensor')
Inputs may be any that keep to these rules, and one draw needn't show every extreme that they name: `block_mask`: each tensor shard's 8 x 32 blocks hold between 64 and 192 kept blocks; in every draw some shard keeps exactly 192.
All inputs are finite; a program needn't handle non-finite values.
Results may differ from a plain program's by a relative error of at most 0.0049.
Values may be sent and summed in bfloat16 or wider, within the bound.
A program may use at most 128 MiB of HBM per device.

v0:
```python
import functools
import math

import jax
import jax.numpy as jnp
from jax import lax
from jax.experimental import pallas as pl
from jax.experimental.pallas import tpu as pltpu
from jax.sharding import PartitionSpec as P

BLOCK = 128
ORDER = (0, 1, 3, 2)
REST = 8


def remote(src, dst, sends, recvs, at, device):
    return pltpu.make_async_remote_copy(
        src_ref=src,
        dst_ref=dst,
        send_sem=sends.at[at],
        recv_sem=recvs.at[at],
        device_id=device,
        device_id_type=pl.DeviceIdType.MESH,
    )


def fused_kernel(
    scale,
    gate_hbm, up_hbm, weight_hbm, mask_ref, grad_hbm,
    out_hbm, gate_grad_hbm, up_grad_hbm, weight_grad_hbm,
    gate, up, weight, cot, hidden, hidden_t, partial,
    first, second, third, send_second, send_third, final,
    rest_third, rest_second, rest_first, send_rest_second, send_rest_first, gate_grad, up_grad, tile_out,
    in_sem, out_sem, tile_sem,
    z_send, z_recv, hop1_send, hop1_recv, hop2_send, hop2_recv, core_send, core_recv,
    sum1_send, sum1_recv, sum2_send, sum2_recv, sum3_send, sum3_recv,
    rest_send, rest_recv, back_send, back_recv,
):
    d = lax.axis_index("dp")
    t = lax.axis_index("tensor")
    x = t % 2
    y = (t // 2) % 2
    z = t // 4
    ff, width = weight.shape
    tokens = gate.shape[0]
    rest = width // REST
    half = (width - rest) // 2
    halves = (pl.ds(0, half), pl.ds(half, half))
    both, last = pl.ds(0, 2 * half), pl.ds(2 * half, rest)
    zs = [z] + [(z + k) % 4 for k in (1, 2, 3)]
    x_peer = {"tensor": z * 4 + y * 2 + (1 - x)}
    y_peer = {"tensor": z * 4 + (1 - y) * 2 + x}
    core_peer = {"dp": 1 - d}
    z_peer = [None] + [{"tensor": zs[k] * 4 + y * 2 + x} for k in (1, 2, 3)]

    loads = [
        pltpu.make_async_copy(gate_hbm, gate, in_sem.at[0]),
        pltpu.make_async_copy(up_hbm, up, in_sem.at[1]),
        pltpu.make_async_copy(weight_hbm.at[:, last], weight.at[:, last], in_sem.at[2]),
        pltpu.make_async_copy(weight_hbm.at[:, both], weight.at[:, both], in_sem.at[3]),
        pltpu.make_async_copy(grad_hbm, cot.at[d, z, y, x], in_sem.at[4]),
    ]
    for copy in loads:
        copy.start()

    barrier = pltpu.get_barrier_semaphore()
    peers = [x_peer, y_peer, core_peer] + z_peer[1:]
    for peer in peers:
        pl.semaphore_signal(barrier, inc=1, device_id=peer, device_id_type=pl.DeviceIdType.MESH)
    pl.semaphore_wait(barrier, len(peers))

    rest_x = remote(
        grad_hbm.at[:, last], cot.at[d, z, y, x, :, last], rest_send, rest_recv, 0, x_peer
    )
    rest_x.start()
    rest_z = {}
    along_z = {}
    for k in (1, 3, 2):
        along_z[k] = remote(
            grad_hbm.at[:, both], cot.at[d, z, y, x, :, both], z_send, z_recv, k - 1, z_peer[k]
        )
        along_z[k].start()
    hop1, hop2, to_core = {}, {}, {}

    def start_hop1(k):
        at = zs[(4 - k) % 4]
        for h, peer in enumerate((x_peer, y_peer)):
            dst = cot.at[d, at, y, x, :, halves[h]]
            src = grad_hbm.at[:, halves[h]] if k == 0 else dst
            hop1[k, h] = remote(src, dst, hop1_send, hop1_recv, 2 * k + h, peer)
            hop1[k, h].start()

    def start_hop2(k):
        at = zs[(4 - k) % 4]
        refs = (cot.at[d, at, y, :, :, halves[0]], cot.at[d, at, :, x, :, halves[1]])
        for h, peer in enumerate((y_peer, x_peer)):
            hop1[k, h].wait_recv()
        for h, peer in enumerate((y_peer, x_peer)):
            hop2[k, h] = remote(refs[h], refs[h], hop2_send, hop2_recv, 2 * k + h, peer)
            hop2[k, h].start()

    def start_core(k):
        at = zs[(4 - k) % 4]
        for h in range(2):
            hop2[k, h].wait_recv()
        if k:
            rest_z[k].wait_recv()
        to_core[k] = remote(cot.at[d, at], cot.at[d, at], core_send, core_recv, k, core_peer)
        to_core[k].start()

    start_hop1(0)

    loads[0].wait()
    loads[1].wait()

    def hidden_step(step, _):
        cols = pl.ds(pl.multiple_of(step * 128, 128), 128)
        g = gate[:, cols].astype(jnp.float32)
        u = up[:, cols].astype(jnp.float32)
        value = g * jax.nn.sigmoid(g) * u
        hidden[:, cols] = value.astype(jnp.bfloat16)
        hidden_t[d, cols, :] = value.T.astype(jnp.bfloat16)
        return 0

    lax.fori_loop(0, ff // 128, hidden_step, 0)
    hidden_core = remote(hidden_t.at[d], hidden_t.at[d], core_send, core_recv, 4, core_peer)
    hidden_core.start()

    def forward(base, size):
        wide = 256

        def step(i, _):
            cols = pl.ds(pl.multiple_of(base + i * wide, BLOCK), wide)
            for b in range(ff // BLOCK):
                rows = pl.ds(b * BLOCK, BLOCK)
                for c in range(wide // BLOCK):
                    at = pl.ds(pl.multiple_of(base + i * wide + c * BLOCK, BLOCK), BLOCK)
                    keep = mask_ref[b, base // BLOCK + i * (wide // BLOCK) + c]
                    keep = jnp.full((BLOCK, BLOCK), keep.astype(jnp.float32)).astype(jnp.bfloat16)
                    weight[rows, at] = weight[rows, at] * keep
            part = jnp.dot(hidden[...], weight[:, cols], preferred_element_type=jnp.float32)
            partial[:, :, :, :, cols] = part.astype(jnp.bfloat16).reshape(
                partial.shape[:4] + (wide,)
            )
            return 0

        lax.fori_loop(0, size // wide, step, 0)

    sum1, sum2, sum3 = {}, {}, {}

    def start_sum1(h):
        for k in (1, 3, 2, 0):
            at = zs[k]
            src = (partial.at[at, :, 1 - x, :, halves[0]], partial.at[at, 1 - y, :, :, halves[1]])[h]
            sum1[k, h] = remote(
                src, first.at[h, k], sum1_send, sum1_recv, 2 * k + h, (x_peer, y_peer)[h]
            )
            sum1[k, h].start()

    back_z = {}

    def rest_sum(row, column):
        total = partial[z, row, column, :, last].astype(jnp.float32)
        for k in (1, 2, 3):
            total = total + rest_third[k - 1, row, column].astype(jnp.float32)
        return total

    loads[4].wait()
    rest_x.wait_recv()
    rest_y = remote(
        cot.at[d, z, y, :, :, last], cot.at[d, z, y, :, :, last], rest_send, rest_recv, 1, y_peer
    )
    rest_y.start()
    loads[2].wait()
    forward(2 * half, rest)
    for k in (1, 3, 2):
        back_z[k] = remote(
            partial.at[zs[k], :, :, :, last], rest_third.at[k - 1], back_send, back_recv, k - 1,
            z_peer[k],
        )
        back_z[k].start()
    loads[3].wait()
    forward(0, half)
    start_sum1(0)
    rest_y.wait_recv()
    for k in (1, 3, 2):
        rest_z[k] = remote(
            cot.at[d, z, :, :, :, last], cot.at[d, z, :, :, :, last], rest_send, rest_recv, k + 1,
            z_peer[k],
        )
        rest_z[k].start()
    for k in (1, 3):
        along_z[k].wait_recv()
        start_hop1(k)
    forward(half, half)
    start_sum1(1)
    along_z[2].wait_recv()
    start_hop1(2)

    def start_sum2(k):
        at = zs[k]
        for h in range(2):
            sum1[k, h].wait_recv()
            other = (1 - y, 1 - x)[h]
            mine = (partial[at, 1 - y, x, :, halves[0]], partial[at, y, 1 - x, :, halves[1]])[h]
            total = mine.astype(jnp.float32) + first[h, k, other].astype(jnp.float32)
            send_second[h, k] = total.astype(jnp.bfloat16)
            sum2[k, h] = remote(
                send_second.at[h, k], second.at[h, k], sum2_send, sum2_recv, 2 * k + h,
                (y_peer, x_peer)[h],
            )
            sum2[k, h].start()

    for k in ORDER:
        start_hop2(k)
    for k in (1, 3, 2):
        start_sum2(k)
    start_sum2(0)
    for k in (1, 2, 3):
        back_z[k].wait_recv()
    for column in range(2):
        send_rest_second[column] = rest_sum(1 - y, column).astype(jnp.bfloat16)
    back_y = remote(send_rest_second, rest_second, back_send, back_recv, 3, y_peer)
    back_y.start()

    def own_total(k, h):
        mine = partial[zs[k], y, x, :, halves[h]].astype(jnp.float32)
        near = first[h, k, (y, x)[h]].astype(jnp.float32)
        return mine + near + second[h, k].astype(jnp.float32)

    def start_sum3(k):
        for h in range(2):
            sum2[k, h].wait_recv()
            send_third[h, k - 1] = own_total(k, h).astype(jnp.bfloat16)
            sum3[k, h] = remote(
                send_third.at[h, k - 1], third.at[h, k - 1], sum3_send, sum3_recv, 2 * k + h - 2,
                z_peer[k],
            )
            sum3[k, h].start()

    start_core(0)
    start_core(1)
    start_core(3)
    start_core(2)
    start_sum3(1)
    start_sum3(3)
    start_sum3(2)
    back_y.wait_recv()
    total = rest_sum(y, 1 - x) + rest_second[1 - x].astype(jnp.float32)
    send_rest_first[...] = total.astype(jnp.bfloat16)
    back_x = remote(send_rest_first, rest_first, back_send, back_recv, 4, x_peer)
    back_x.start()

    def grad_step(i, _):
        wide = 256
        rows = pl.ds(pl.multiple_of(i * wide, wide), wide)
        rows_out = cot[d].reshape(tokens, width)
        back = lax.dot_general(
            rows_out, weight[rows, :], (((1,), (1,)), ((), ())), preferred_element_type=jnp.float32
        )
        g = gate[:, rows].astype(jnp.float32)
        u = up[:, rows].astype(jnp.float32)
        s = jax.nn.sigmoid(g)
        gate_grad[:, rows] = (back * u * s * (1.0 + g * (1.0 - s))).astype(jnp.bfloat16)
        up_grad[:, rows] = (back * (g * s)).astype(jnp.bfloat16)
        return 0

    lax.fori_loop(0, ff // 256, grad_step, 0)
    stores = [
        pltpu.make_async_copy(gate_grad, gate_grad_hbm, out_sem.at[0]),
        pltpu.make_async_copy(up_grad, up_grad_hbm, out_sem.at[1]),
    ]
    for copy in stores:
        copy.start()

    hidden_core.wait_recv()
    for k in ORDER:
        to_core[k].wait_recv()

    wide = 512

    def tile_copy(slot, i):
        cols = pl.ds(pl.multiple_of(i * wide, wide), wide)
        return pltpu.make_async_copy(
            tile_out.at[slot], weight_grad_hbm.at[:, cols], tile_sem.at[slot]
        )

    def weight_step(j, _):
        for slot in range(2):
            i = 2 * j + slot
            cols = pl.ds(pl.multiple_of(i * wide, wide), wide)

            @pl.when(j > 0)
            def _():
                tile_copy(slot, i - 2).wait()

            total = jnp.zeros((ff, wide), jnp.float32)
            for core in range(2):
                total = total + jnp.dot(
                    hidden_t[core],
                    cot[core, :, :, :, :, cols].reshape(tokens, wide),
                    preferred_element_type=jnp.float32,
                )
            for b in range(ff // BLOCK):
                for c in range(wide // BLOCK):
                    keep = mask_ref[b, i * (wide // BLOCK) + c].astype(jnp.float32) * scale
                    block = total[b * BLOCK : (b + 1) * BLOCK, c * BLOCK : (c + 1) * BLOCK]
                    tile_out[slot, pl.ds(b * BLOCK, BLOCK), pl.ds(c * BLOCK, BLOCK)] = (
                        block * keep
                    ).astype(jnp.bfloat16)
            tile_copy(slot, i).start()
        return 0

    steps = width // wide
    lax.fori_loop(0, steps // 2, weight_step, 0)

    for h in range(2):
        sum2[0, h].wait_recv()
        total = own_total(0, h)
        for k in (1, 2, 3):
            sum3[k, h].wait_recv()
            total = total + third[h, k - 1].astype(jnp.float32)
        final[:, halves[h]] = total.astype(jnp.bfloat16)
    back_x.wait_recv()
    total = rest_sum(y, x) + rest_second[x].astype(jnp.float32) + rest_first[...].astype(jnp.float32)
    final[:, last] = total.astype(jnp.bfloat16)
    stores.append(pltpu.make_async_copy(final, out_hbm, out_sem.at[2]))
    stores[-1].start()

    for copies in (along_z, hop1, hop2, to_core, sum1, sum2, sum3, rest_z, back_z):
        for copy in copies.values():
            copy.wait_send()
    for copy in (hidden_core, rest_x, rest_y, back_y, back_x):
        copy.wait_send()
    for copy in stores:
        copy.wait()
    tile_copy(0, steps - 2).wait()
    tile_copy(1, steps - 1).wait()


def fused(gate_pre, up_pre, down_weight, block_mask, out_grad):
    tokens, ff = gate_pre.shape
    rows, width = out_grad.shape
    rest = width // REST
    half = (width - rest) // 2
    scale = 1.0 / math.sqrt(tokens * 2)
    hbm = pl.BlockSpec(memory_space=pl.ANY)
    bf16 = jnp.bfloat16
    dma = pltpu.SemaphoreType.DMA
    counts = [3, 8, 8, 5, 8, 8, 6, 5, 5]
    results = pl.pallas_call(
        functools.partial(fused_kernel, scale),
        out_shape=(
            jax.ShapeDtypeStruct((rows, width), bf16),
            jax.ShapeDtypeStruct((tokens, ff), bf16),
            jax.ShapeDtypeStruct((tokens, ff), bf16),
            jax.ShapeDtypeStruct((ff, width), bf16),
        ),
        in_specs=[hbm, hbm, hbm, pl.BlockSpec(memory_space=pltpu.SMEM), hbm],
        out_specs=(hbm,) * 4,
        scratch_shapes=[
            pltpu.VMEM((tokens, ff), bf16),
            pltpu.VMEM((tokens, ff), bf16),
            pltpu.VMEM((ff, width), bf16),
            pltpu.VMEM((2, 4, 2, 2, rows, width), bf16),
            pltpu.VMEM((tokens, ff), bf16),
            pltpu.VMEM((2, ff, tokens), bf16),
            pltpu.VMEM((4, 2, 2, rows, width), bf16),
            pltpu.VMEM((2, 4, 2, rows, half), bf16),
            pltpu.VMEM((2, 4, rows, half), bf16),
            pltpu.VMEM((2, 3, rows, half), bf16),
            pltpu.VMEM((2, 4, rows, half), bf16),
            pltpu.VMEM((2, 3, rows, half), bf16),
            pltpu.VMEM((rows, width), bf16),
            pltpu.VMEM((3, 2, 2, rows, rest), bf16),
            pltpu.VMEM((2, rows, rest), bf16),
            pltpu.VMEM((rows, rest), bf16),
            pltpu.VMEM((2, rows, rest), bf16),
            pltpu.VMEM((rows, rest), bf16),
            pltpu.VMEM((tokens, ff), bf16),
            pltpu.VMEM((tokens, ff), bf16),
            pltpu.VMEM((2, ff, 512), bf16),
            dma((5,)),
            dma((3,)),
            dma((2,)),
        ]
        + [dma((count,)) for count in counts for _ in range(2)],
        compiler_params=pltpu.CompilerParams(
            collective_id=0, has_side_effects=True, vmem_limit_bytes=60 * 2**20
        ),
        cost_estimate=pl.CostEstimate(
            flops=8 * tokens * ff * width, bytes_accessed=40 * 2**20, transcendentals=2 * tokens * ff
        ),
    )(gate_pre, up_pre, down_weight, block_mask, out_grad)
    return hand_on(results)


def pieces_of(array):
    count = max(1, array.size // 2**19)
    return [(piece * (array.shape[0] // count), array.shape[0] // count) for piece in range(count)]


def hand_on_kernel(arrays, *refs):
    srcs, dsts = refs[:arrays], refs[arrays : 2 * arrays]
    held = refs[2 * arrays : 3 * arrays]
    load_sem, store_sem = refs[3 * arrays :]
    loads, stores = [], []
    for src, dst, hold in zip(srcs, dsts, held):
        for first_row, rows in pieces_of(src):
            at = pl.ds(first_row, rows)
            n = len(loads)
            loads.append(pltpu.make_async_copy(src.at[at], hold.at[at], load_sem.at[n]))
            stores.append(pltpu.make_async_copy(hold.at[at], dst.at[at], store_sem.at[n]))
    for load in loads:
        load.start()
    for load, store in zip(loads, stores):
        load.wait()
        store.start()
    for store in stores:
        store.wait()


def hand_on(arrays):
    hbm = pl.BlockSpec(memory_space=pl.ANY)
    count = sum(len(pieces_of(a)) for a in arrays)
    return pl.pallas_call(
        functools.partial(hand_on_kernel, len(arrays)),
        out_shape=tuple(jax.ShapeDtypeStruct(a.shape, a.dtype) for a in arrays),
        in_specs=[hbm] * len(arrays),
        out_specs=(hbm,) * len(arrays),
        scratch_shapes=[pltpu.VMEM(a.shape, a.dtype) for a in arrays]
        + [pltpu.SemaphoreType.DMA((count,))] * 2,
        compiler_params=pltpu.CompilerParams(vmem_limit_bytes=60 * 2**20),
    )(*arrays)


def local(gate_pre, up_pre, down_weight, block_mask, out_grad):
    blk_rows, blk_cols = block_mask.shape
    ff_local, width = down_weight.shape
    masked = (
        down_weight.reshape(blk_rows, 128, blk_cols, 128)
        * block_mask.astype(jnp.bfloat16)[:, None, :, None]
    ).reshape(ff_local, width)
    gate_val = gate_pre.astype(jnp.float32)
    up_val = up_pre.astype(jnp.float32)
    sigmoid_gate = jax.nn.sigmoid(gate_val)
    silu_gate = gate_val * sigmoid_gate
    hidden = (silu_gate * up_val).astype(jnp.bfloat16)
    layer_out = lax.psum_scatter(
        jnp.dot(hidden, masked, preferred_element_type=jnp.float32),
        "tensor",
        scatter_dimension=0,
        tiled=True,
    ).astype(jnp.bfloat16)
    cot_rows = lax.all_gather(out_grad, "tensor", axis=0, tiled=True)
    hidden_grad = lax.dot_general(
        cot_rows, masked, (((1,), (1,)), ((), ())), preferred_element_type=jnp.float32
    )
    gate_grad = (
        hidden_grad * up_val * sigmoid_gate * (1.0 + gate_val * (1.0 - sigmoid_gate))
    ).astype(jnp.bfloat16)
    up_grad = (hidden_grad * silu_gate).astype(jnp.bfloat16)
    tokens_all = out_grad.shape[0] * lax.axis_size("tensor") * lax.axis_size("dp")
    grad_scale = 1.0 / math.sqrt(tokens_all)
    partial_grad = (
        lax.dot_general(
            hidden, cot_rows, (((0,), (0,)), ((), ())), preferred_element_type=jnp.float32
        )
        * grad_scale
    )
    blocked = (
        partial_grad.reshape(blk_rows, 128, blk_cols, 128)
        * block_mask.astype(jnp.float32)[:, None, :, None]
    )
    summed = lax.psum(blocked.reshape(ff_local, width), "dp")
    weight_grad = summed.astype(jnp.bfloat16)
    return (layer_out, gate_grad, up_grad, weight_grad)


def solution(mesh):
    grouped = mesh.shape["dp"] == 2 and mesh.shape["tensor"] == 16
    return jax.shard_map(
        fused if grouped else local,
        mesh=mesh,
        in_specs=(
            P("dp", "tensor"),
            P("dp", "tensor"),
            P("tensor", None),
            P("tensor", None),
            P(("dp", "tensor"), None),
        ),
        out_specs=(
            P(("dp", "tensor"), None),
            P("dp", "tensor"),
            P("dp", "tensor"),
            P("tensor", None),
        ),
        check_vma=False,
    )
```

profile of v0, /device:TPU:0, one launch (start us, length us, event | category | flops | bytes accessed | tf_op | source)
XLA Modules:
  0.0 102.9 jit_solution(5318453669607567242)
XLA Ops:
  0.6 93.9 %shard_map.84 = (bf16[32,4096]{1,0:T(8,128)(2,1)}, bf16[512,1024]{1,0:T(8,128)(2,1)}, bf16[512,1024]{1,0:T(8,128)(2,1)}, bf16[1024,4096]{1,0:T(8,128)(2,1)}) custom-call(bf16[512,1024]{1,0:T(8,128)(2,1)} %gate_hbm.1, bf16[512,1024]{1,0:T(8,128)(2,1)} %up_hbm.1, bf16[1024,4096]{1,0:T(8,128)(2,1)} %weight_hbm.1, s32[8,32]{1,0:T(8,128)} %mask_ref.1, ...), custom_call_target="tpu_custom_call" | custom-call | flops 17179869184 | bytes 41943040 | tf_op jit(solution)/shard_map/pallas_call | solution.py:351
  94.5 8.4 %shard_map.85 = (bf16[32,4096]{1,0:T(8,128)(2,1)}, bf16[512,1024]{1,0:T(8,128)(2,1)}, bf16[512,1024]{1,0:T(8,128)(2,1)}, bf16[1024,4096]{1,0:T(8,128)(2,1)}) custom-call(bf16[32,4096]{1,0:T(8,128)(2,1)} %get-tuple-element.8.refs_0_, bf16[512,1024]{1,0:T(8,128)(2,1)} %get-tuple-element.9.refs_1_, bf16[512,1024]{1,0:T(8,128)(2,1)} %get-tuple-element.10.refs_2_, ...), custom_call_target="tpu_custom_call" | custom-call | tf_op jit(solution)/shard_map/pallas_call | solution.py:426
where the time goes:
time: 103 us
  Pallas kernels  102 us (99%)
    pallas_call x1, Pallas kernels, fused(): pl.pallas_call(functools.partial(fused_kernel, scale), out_shape=(jax.Sha...  93.9 us
    pallas_call x1, Pallas kernels, hand_on(): pl.pallas_call(functools.partial(hand_on_kernel, len(arrays)), out_shape=...  8.37 us

commit v1 on v0

--- a/solution.py
+++ b/solution.py
@@ -27,11 +27,11 @@
 def fused_kernel(
     scale,
     gate_hbm, up_hbm, weight_hbm, mask_ref, grad_hbm,
-    out_hbm, gate_grad_hbm, up_grad_hbm, weight_grad_hbm,
+    final, gate_grad, up_grad, weight_grad,
     gate, up, weight, cot, hidden, hidden_t, partial,
-    first, second, third, send_second, send_third, final,
-    rest_third, rest_second, rest_first, send_rest_second, send_rest_first, gate_grad, up_grad, tile_out,
-    in_sem, out_sem, tile_sem,
+    first, second, third, send_second, send_third,
+    rest_third, rest_second, rest_first, send_rest_second, send_rest_first,
+    in_sem,
     z_send, z_recv, hop1_send, hop1_recv, hop2_send, hop2_recv, core_send, core_recv,
     sum1_send, sum1_recv, sum2_send, sum2_recv, sum3_send, sum3_recv,
     rest_send, rest_recv, back_send, back_recv,
@@ -266,53 +266,30 @@
         return 0
 
     lax.fori_loop(0, ff // 256, grad_step, 0)
-    stores = [
-        pltpu.make_async_copy(gate_grad, gate_grad_hbm, out_sem.at[0]),
-        pltpu.make_async_copy(up_grad, up_grad_hbm, out_sem.at[1]),
-    ]
-    for copy in stores:
-        copy.start()
-
     hidden_core.wait_recv()
     for k in ORDER:
         to_core[k].wait_recv()
 
     wide = 512
 
-    def tile_copy(slot, i):
+    def weight_step(i, _):
         cols = pl.ds(pl.multiple_of(i * wide, wide), wide)
-        return pltpu.make_async_copy(
-            tile_out.at[slot], weight_grad_hbm.at[:, cols], tile_sem.at[slot]
-        )
-
-    def weight_step(j, _):
-        for slot in range(2):
-            i = 2 * j + slot
-            cols = pl.ds(pl.multiple_of(i * wide, wide), wide)
-
-            @pl.when(j > 0)
-            def _():
-                tile_copy(slot, i - 2).wait()
-
-            total = jnp.zeros((ff, wide), jnp.float32)
-            for core in range(2):
-                total = total + jnp.dot(
-                    hidden_t[core],
-                    cot[core, :, :, :, :, cols].reshape(tokens, wide),
-                    preferred_element_type=jnp.float32,
-                )
-            for b in range(ff // BLOCK):
-                for c in range(wide // BLOCK):
-                    keep = mask_ref[b, i * (wide // BLOCK) + c].astype(jnp.float32) * scale
-                    block = total[b * BLOCK : (b + 1) * BLOCK, c * BLOCK : (c + 1) * BLOCK]
-                    tile_out[slot, pl.ds(b * BLOCK, BLOCK), pl.ds(c * BLOCK, BLOCK)] = (
-                        block * keep
-                    ).astype(jnp.bfloat16)
-            tile_copy(slot, i).start()
+        total = jnp.zeros((ff, wide), jnp.float32)
+        for core in range(2):
+            total = total + jnp.dot(
+                hidden_t[core],
+                cot[core, :, :, :, :, cols].reshape(tokens, wide),
+                preferred_element_type=jnp.float32,
+            )
+        for b in range(ff // BLOCK):
+            for c in range(wide // BLOCK):
+                keep = mask_ref[b, i * (wide // BLOCK) + c].astype(jnp.float32) * scale
+                block = total[b * BLOCK : (b + 1) * BLOCK, c * BLOCK : (c + 1) * BLOCK]
+                at = pl.ds(pl.multiple_of(i * wide + c * BLOCK, BLOCK), BLOCK)
+                weight_grad[pl.ds(b * BLOCK, BLOCK), at] = (block * keep).astype(jnp.bfloat16)
         return 0
 
-    steps = width // wide
-    lax.fori_loop(0, steps // 2, weight_step, 0)
+    lax.fori_loop(0, width // wide, weight_step, 0)
 
     for h in range(2):
         sum2[0, h].wait_recv()
@@ -324,18 +301,16 @@
     back_x.wait_recv()
     total = rest_sum(y, x) + rest_second[x].astype(jnp.float32) + rest_first[...].astype(jnp.float32)
     final[:, last] = total.astype(jnp.bfloat16)
-    stores.append(pltpu.make_async_copy(final, out_hbm, out_sem.at[2]))
-    stores[-1].start()
 
     for copies in (along_z, hop1, hop2, to_core, sum1, sum2, sum3, rest_z, back_z):
         for copy in copies.values():
             copy.wait_send()
     for copy in (hidden_core, rest_x, rest_y, back_y, back_x):
         copy.wait_send()
-    for copy in stores:
-        copy.wait()
-    tile_copy(0, steps - 2).wait()
-    tile_copy(1, steps - 1).wait()
+
+
+def keep_in_hbm(array):
+    return pltpu.with_memory_space_constraint(array, pltpu.HBM)
 
 
 def fused(gate_pre, up_pre, down_weight, block_mask, out_grad):
@@ -351,13 +326,13 @@
     results = pl.pallas_call(
         functools.partial(fused_kernel, scale),
         out_shape=(
-            jax.ShapeDtypeStruct((rows, width), bf16),
-            jax.ShapeDtypeStruct((tokens, ff), bf16),
-            jax.ShapeDtypeStruct((tokens, ff), bf16),
-            jax.ShapeDtypeStruct((ff, width), bf16),
+            pltpu.VMEM((rows, width), bf16),
+            pltpu.VMEM((tokens, ff), bf16),
+            pltpu.VMEM((tokens, ff), bf16),
+            pltpu.VMEM((ff, width), bf16),
         ),
         in_specs=[hbm, hbm, hbm, pl.BlockSpec(memory_space=pltpu.SMEM), hbm],
-        out_specs=(hbm,) * 4,
+        out_specs=(pl.BlockSpec(memory_space=pltpu.VMEM),) * 4,
         scratch_shapes=[
             pltpu.VMEM((tokens, ff), bf16),
             pltpu.VMEM((tokens, ff), bf16),
@@ -371,67 +346,45 @@
             pltpu.VMEM((2, 3, rows, half), bf16),
             pltpu.VMEM((2, 4, rows, half), bf16),
             pltpu.VMEM((2, 3, rows, half), bf16),
-            pltpu.VMEM((rows, width), bf16),
             pltpu.VMEM((3, 2, 2, rows, rest), bf16),
             pltpu.VMEM((2, rows, rest), bf16),
             pltpu.VMEM((rows, rest), bf16),
             pltpu.VMEM((2, rows, rest), bf16),
             pltpu.VMEM((rows, rest), bf16),
-            pltpu.VMEM((tokens, ff), bf16),
-            pltpu.VMEM((tokens, ff), bf16),
-            pltpu.VMEM((2, ff, 512), bf16),
             dma((5,)),
-            dma((3,)),
-            dma((2,)),
         ]
         + [dma((count,)) for count in counts for _ in range(2)],
         compiler_params=pltpu.CompilerParams(
-            collective_id=0, has_side_effects=True, vmem_limit_bytes=60 * 2**20
+            collective_id=0, has_side_effects=True, vmem_limit_bytes=50 * 2**20
         ),
         cost_estimate=pl.CostEstimate(
             flops=8 * tokens * ff * width, bytes_accessed=40 * 2**20, transcendentals=2 * tokens * ff
         ),
-    )(gate_pre, up_pre, down_weight, block_mask, out_grad)
+    )(*(keep_in_hbm(a) for a in (gate_pre, up_pre, down_weight)), block_mask, keep_in_hbm(out_grad))
     return hand_on(results)
 
 
-def pieces_of(array):
-    count = max(1, array.size // 2**19)
-    return [(piece * (array.shape[0] // count), array.shape[0] // count) for piece in range(count)]
-
-
 def hand_on_kernel(arrays, *refs):
-    srcs, dsts = refs[:arrays], refs[arrays : 2 * arrays]
-    held = refs[2 * arrays : 3 * arrays]
-    load_sem, store_sem = refs[3 * arrays :]
-    loads, stores = [], []
-    for src, dst, hold in zip(srcs, dsts, held):
-        for first_row, rows in pieces_of(src):
-            at = pl.ds(first_row, rows)
-            n = len(loads)
-            loads.append(pltpu.make_async_copy(src.at[at], hold.at[at], load_sem.at[n]))
-            stores.append(pltpu.make_async_copy(hold.at[at], dst.at[at], store_sem.at[n]))
-    for load in loads:
-        load.start()
-    for load, store in zip(loads, stores):
-        load.wait()
+    srcs, dsts, store_sem = refs[:arrays], refs[arrays : 2 * arrays], refs[2 * arrays]
+    stores = [
+        pltpu.make_async_copy(src, dst, store_sem.at[n])
+        for n, (src, dst) in enumerate(zip(srcs, dsts))
+    ]
+    for store in stores:
         store.start()
     for store in stores:
         store.wait()
 
 
 def hand_on(arrays):
-    hbm = pl.BlockSpec(memory_space=pl.ANY)
-    count = sum(len(pieces_of(a)) for a in arrays)
     return pl.pallas_call(
         functools.partial(hand_on_kernel, len(arrays)),
         out_shape=tuple(jax.ShapeDtypeStruct(a.shape, a.dtype) for a in arrays),
-        in_specs=[hbm] * len(arrays),
-        out_specs=(hbm,) * len(arrays),
-        scratch_shapes=[pltpu.VMEM(a.shape, a.dtype) for a in arrays]
-        + [pltpu.SemaphoreType.DMA((count,))] * 2,
-        compiler_params=pltpu.CompilerParams(vmem_limit_bytes=60 * 2**20),
-    )(*arrays)
+        in_specs=[pl.BlockSpec(memory_space=pltpu.VMEM)] * len(arrays),
+        out_specs=(pl.BlockSpec(memory_space=pl.ANY),) * len(arrays),
+        scratch_shapes=[pltpu.SemaphoreType.DMA((len(arrays),))],
+        compiler_params=pltpu.CompilerParams(vmem_limit_bytes=2 * 2**20),
+    )(*(pltpu.with_memory_space_constraint(a, pltpu.VMEM) for a in arrays))
 
 
 def local(gate_pre, up_pre, down_weight, block_mask, out_grad):

time: 103 us -> 98.7 us (0.958)
  Pallas kernels: 102 us -> 97.8 us
    pallas_call x1, Pallas kernels: 8.37 us -> 4.21 us  [hand_on(): pl.pallas_call(functools.partial(hand_on_kernel, len(arrays)), out_shape=...]
where the time goes in v1:
time: 98.7 us; the launch traced here: 98.5 us
  Pallas kernels  97.8 us (99%)
    pallas_call x1, Pallas kernels, fused(): pl.pallas_call(functools.partial(fused_kernel, scale), out_shape=(pltpu.V...  93.6 us
    pallas_call x1, Pallas kernels, hand_on(): pl.pallas_call(functools.partial(hand_on_kernel, len(arrays)), out_shape=...  4.21 us

profile of v1, /device:TPU:0, one launch (start us, length us, event | category | flops | bytes accessed | tf_op | source)
XLA Modules:
  0.0 98.5 jit_solution(16842107803039700752)
XLA Ops:
  0.6 93.6 %shard_map.84 = (bf16[32,4096]{1,0:T(8,128)(2,1)S(1)}, bf16[512,1024]{1,0:T(8,128)(2,1)S(1)}, bf16[512,1024]{1,0:T(8,128)(2,1)S(1)}, bf16[1024,4096]{1,0:T(8,128)(2,1)S(1)}) custom-call(bf16[512,1024]{1,0:T(8,128)(2,1)} %gate_hbm.1, bf16[512,1024]{1,0:T(8,128)(2,1)} %up_hbm.1, bf16[1024,4096]{1,0:T(8,128)(2,1)} %weight_hbm.1, s32[8,32]{1,0:T(8,128)} %mask_ref.1, ...), custom_call_target="tpu_custom_call" | custom-call | flops 17179869184 | bytes 41943040 | tf_op jit(solution)/shard_map/pallas_call | solution.py:326
  94.3 4.2 %shard_map.85 = (bf16[32,4096]{1,0:T(8,128)(2,1)}, bf16[512,1024]{1,0:T(8,128)(2,1)}, bf16[512,1024]{1,0:T(8,128)(2,1)}, bf16[1024,4096]{1,0:T(8,128)(2,1)}) custom-call(bf16[32,4096]{1,0:T(8,128)(2,1)S(1)} %get-tuple-element.8.refs_0_, bf16[512,1024]{1,0:T(8,128)(2,1)S(1)} %get-tuple-element.9.refs_1_, bf16[512,1024]{1,0:T(8,128)(2,1)S(1)} %get-tuple-element.10.refs_2_, ...), custom_call_target="tpu_custom_call" | custom-call | tf_op jit(solution)/shard_map/pallas_call | solution.py:380

commit v2 on v1

v2 whole, which is shorter than its diff:
```python
import functools
import math

import jax
import jax.numpy as jnp
from jax import lax
from jax.experimental import pallas as pl
from jax.experimental.pallas import tpu as pltpu
from jax.sharding import PartitionSpec as P

BLOCK = 128
STEP = 512
CHUNKS = (("z", 1), ("z", 2), ("z", 2), ("x", 1), ("x", 1), ("x", 1))
CHUNK_SCRATCH = 5


FORWARD = (0, 1, 5, 4, 3, 2)
PLAN = (
    ("gather", 1), ("hop1", 5, 0), ("hop1", 4, 0), ("hop1", 3, 0), ("gather", 0), ("own",),
    ("hop1", 1, 0), ("hop1", 2, 0), ("hop2", 5, 0), ("hop2", 4, 0), ("loads",), ("hop1", 0, 0),
    ("hop2", 3, 0), ("pass", 1, 0), ("pass", 1, 1), ("gather", 2), ("hop1", 1, 1), ("hop1", 1, 2),
    ("hop2", 1, 0), ("hidden",), ("hop2", 2, 0), ("square", 5, 0), ("core", 5, 0), ("pass", 1, 2),
    ("pass", 0, 0), ("gather", 5), ("fwd", 0, 0), ("sum1", 0, 3), ("pass", 2, 0), ("pass", 0, 1),
    ("hop1", 1, 3), ("hop1", 0, 1), ("fwd", 1, 0), ("square", 4, 0), ("gather", 4),
    ("hop2", 1, 2), ("hop1", 0, 2), ("hop2", 1, 1), ("fwd", 1, 1), ("hop1", 2, 1),
    ("square", 2, 0), ("square", 1, 0), ("square", 3, 0), ("hop2", 1, 3), ("core", 4, 0),
    ("gather", 3), ("sum1", 0, 1), ("pass", 5, 0), ("core", 2, 0), ("fwd", 5, 0), ("fwd", 4, 0),
    ("sum1", 1, 2), ("hop2", 0, 2), ("hop2", 0, 0), ("sum2", 0, 3), ("core", 1, 0),
    ("square", 1, 2), ("core", 1, 2), ("pass", 4, 0), ("core", 3, 0), ("core", 5, 1),
    ("square", 1, 1), ("hop2", 0, 1), ("sum1", 0, 0), ("core", 4, 1), ("pass", 2, 1),
    ("hop1", 2, 2), ("sumz", 5, 3), ("hop2", 2, 1), ("sum1", 0, 2), ("fwd", 3, 0),
    ("square", 1, 3), ("core", 1, 3), ("core", 1, 1), ("hg", 1, 0), ("sum2", 0, 1),
    ("pass", 3, 0), ("sumz", 3, 3), ("fwd", 2, 0), ("sum1", 1, 1), ("square", 0, 2),
    ("core", 3, 1), ("fwd", 2, 1), ("pass", 5, 1), ("sum2", 1, 2), ("sumz", 4, 3), ("pass", 2, 2),
    ("pass", 3, 1), ("core", 0, 2), ("sumz", 5, 2), ("total", 0, 3), ("hop1", 2, 3), ("hg", 1, 1),
    ("sum1", 1, 0), ("hcore",), ("wg", 1, 0), ("hop2", 2, 2), ("core", 3, 2), ("total", 1, 2),
    ("pass", 4, 1), ("sum2", 1, 1), ("hop2", 2, 3), ("sum2", 0, 2), ("core", 5, 2),
    ("sum1", 2, 1), ("sum1", 2, 2), ("sum1", 2, 3), ("core", 4, 2), ("square", 2, 1),
    ("square", 0, 0), ("pass", 5, 2), ("sumz", 3, 2), ("core", 2, 1), ("core", 0, 0),
    ("sum2", 0, 0), ("hg", 5, 0), ("core", 5, 3), ("sum1", 1, 3), ("wg", 1, 1), ("sum2", 1, 0),
    ("sum1", 2, 0), ("sumz", 4, 2), ("sumz", 5, 1), ("square", 2, 2), ("wg", 5, 0),
    ("core", 2, 2), ("total", 0, 1), ("square", 0, 1), ("square", 2, 3), ("core", 2, 3),
    ("hg", 2, 0), ("hg", 2, 1), ("wg", 2, 0), ("pass", 0, 2), ("hop1", 0, 3), ("sumz", 3, 1),
    ("sum2", 2, 2), ("hg", 5, 1), ("core", 0, 1), ("sum2", 2, 3), ("pass", 4, 2), ("sum2", 2, 1),
    ("total", 1, 1), ("hg", 4, 0), ("sum2", 1, 3), ("hg", 4, 1), ("sumz", 4, 1), ("wg", 2, 1),
    ("total", 0, 2), ("hop2", 0, 3), ("pass", 3, 2), ("line", 3), ("line", 5), ("sum1", 5, 0),
    ("sum1", 3, 0), ("total", 2, 3), ("line", 4), ("sum1", 4, 0), ("total", 2, 1),
    ("total", 1, 3), ("sum2", 2, 0), ("total", 2, 2), ("core", 4, 3), ("sumz", 0, 3),
    ("hg", 3, 0), ("core", 3, 3), ("sumz", 2, 3), ("square", 0, 3), ("hg", 0, 0), ("core", 0, 3),
    ("sumz", 1, 3), ("sum2", 4, 0), ("sumz", 0, 2), ("sum2", 3, 0), ("sum2", 5, 0), ("hg", 3, 1),
    ("sumz", 2, 2), ("sumz", 0, 1), ("hg", 0, 1), ("sumz", 1, 2), ("sumz", 2, 1), ("endx", 4),
    ("wg", 4, 0), ("sumz", 1, 1), ("endx", 5), ("wg", 3, 0), ("endx", 3), ("endz", 0),
    ("wg", 0, 0), ("endz", 2), ("endz", 1),
)


def remote(src, dst, send, recv, device):
    return pltpu.make_async_remote_copy(
        src_ref=src,
        dst_ref=dst,
        send_sem=send,
        recv_sem=recv,
        device_id=device,
        device_id_type=pl.DeviceIdType.MESH,
    )


def chunk_columns(width):
    unit = width // 8
    at, spans = 0, []
    for _, units in CHUNKS:
        spans.append((at, units * unit))
        at += units * unit
    return spans


def f32(value):
    return value.astype(jnp.float32)


def fused_kernel(
    scale,
    gate_hbm, up_hbm, weight_hbm, mask_ref, grad_hbm,
    final, gate_grad, up_grad, weight_grad,
    gate, up, weight, cot, hidden, hidden_t, partial, acc,
    in_sem, weight_sem, hidden_send, hidden_recv,
    *scratch,
):
    d = lax.axis_index("dp")
    t = lax.axis_index("tensor")
    x = t % 2
    y = (t // 2) % 2
    z = t // 4
    ff, width = weight.shape
    tokens = gate.shape[0]
    bf16 = jnp.bfloat16
    spans = chunk_columns(width)

    mid = ((z + 1) // 2) % 2
    end = 1 - mid
    is_mid = mid == 1
    inner = mid * (3 - z) + end * (1 + z // 3)
    outer = mid * (z - 1) * 3
    far = end * (3 - z) + mid * (2 - z) * 3
    blocks = (z, inner, end * (3 - inner) + mid * outer, far)

    def along(level):
        return {"tensor": level * 4 + y * 2 + x}

    x_peer = {"tensor": z * 4 + y * 2 + (1 - x)}
    y_peer = {"tensor": z * 4 + (1 - y) * 2 + x}
    core_peer = {"dp": 1 - d}
    inner_peer, outer_peer = along(inner), along(outer)

    loads = [
        pltpu.make_async_copy(gate_hbm, gate, in_sem.at[0]),
        pltpu.make_async_copy(up_hbm, up, in_sem.at[1]),
        pltpu.make_async_copy(grad_hbm, cot.at[d, z, y, x], in_sem.at[2]),
    ]
    weight_loads = {}
    for c, (at, size) in enumerate(spans):
        cols = pl.ds(at, size)
        weight_loads[c] = pltpu.make_async_copy(
            weight_hbm.at[:, cols], weight.at[:, cols], weight_sem.at[c]
        )
    for copy in loads:
        copy.start()
    for c in FORWARD:
        weight_loads[c].start()

    barrier = pltpu.get_barrier_semaphore()
    for peer in (x_peer, y_peer, core_peer, inner_peer):
        pl.semaphore_signal(barrier, inc=1, device_id=peer, device_id_type=pl.DeviceIdType.MESH)

    @pl.when(is_mid)
    def _():
        pl.semaphore_signal(
            barrier, inc=1, device_id=outer_peer, device_id_type=pl.DeviceIdType.MESH
        )

    pl.semaphore_wait(barrier, 4 + mid)

    hidden_core = remote(
        hidden_t.at[d], hidden_t.at[d], hidden_send.at[0], hidden_recv.at[0], core_peer
    )
    sent = []
    sent_mid = []

    def go(copy):
        copy.start()
        sent.append(copy)
        return copy

    class Chunk:
        pass

    def both_halves(chunk):
        return ((0, x_peer, y_peer, chunk.halves[0]), (1, y_peer, x_peer, chunk.halves[1]))

    chunks = []
    for c, (kind, _) in enumerate(CHUNKS):
        chunk = Chunk()
        at, size = spans[c]
        chunk.kind, chunk.at, chunk.size = kind, at, size
        chunk.cols = pl.ds(at, size)
        chunk.halves = (pl.ds(at, size // 2), pl.ds(at + size // 2, size // 2))
        chunk.first, chunk.second, chunk.along, chunk.send, chunk.recv = scratch[
            CHUNK_SCRATCH * c : CHUNK_SCRATCH * (c + 1)
        ]
        chunk.hop1, chunk.hop2, chunk.core, chunk.sum1, chunk.sum2 = {}, {}, {}, {}, {}
        chunks.append(chunk)


    def piece(chunk, b):
        if chunk.kind == "z":
            return cot.at[d, b, y, x, :, chunk.cols]
        return cot.at[d, b, :, :, :, chunk.cols]

    def gather_z(chunk):
        own = piece(chunk, z)
        src = grad_hbm.at[:, chunk.cols] if chunk.kind == "z" else own
        go(remote(src, own, chunk.send.at[36], chunk.recv.at[36 + end], inner_peer))

        @pl.when(is_mid)
        def _():
            remote(src, own, chunk.send.at[37], chunk.recv.at[36], outer_peer).start()

        sent_mid.append(remote(src, own, chunk.send.at[37], chunk.recv.at[36], outer_peer))

    def pass_z(chunk, s):
        block = piece(chunk, blocks[s + 1])
        remote(block, block, chunk.send.at[36], chunk.recv.at[36 + s], inner_peer).wait_recv()
        to, slot = ((outer_peer, 1), (inner_peer, 2), (outer_peer, 2))[s]
        copy = remote(block, block, chunk.send.at[38 + s], chunk.recv.at[36 + slot], to)

        @pl.when(is_mid)
        def _():
            copy.start()

        sent_mid.append(copy)

    def hop1(chunk, k):
        for h, near, _, half in both_halves(chunk):
            dst = cot.at[d, blocks[k], y, x, :, half]
            src = grad_hbm.at[:, half] if k == 0 else dst
            n = 2 * k + h
            chunk.hop1[k, h] = go(remote(src, dst, chunk.send.at[n], chunk.recv.at[n], near))

    def hop2(chunk, k):
        for h in range(2):
            chunk.hop1[k, h].wait_recv()
        for h, _, other, half in both_halves(chunk):
            ref = (cot.at[d, blocks[k], y, :, :, half], cot.at[d, blocks[k], :, x, :, half])[h]
            n = 8 + 2 * k + h
            chunk.hop2[k, h] = go(remote(ref, ref, chunk.send.at[n], chunk.recv.at[n], other))

    def square(chunk, k):
        for h in range(2):
            chunk.hop2[k, h].wait_recv()

    def to_core(chunk, k):
        ref = cot.at[d, blocks[k], :, :, :, chunk.cols]
        chunk.core[k] = go(
            remote(ref, ref, chunk.send.at[16 + k], chunk.recv.at[16 + k], core_peer)
        )

    def sum1(chunk, k):
        for h, near, _, half in both_halves(chunk):
            src = (
                partial.at[blocks[k], :, 1 - x, :, half],
                partial.at[blocks[k], 1 - y, :, :, half],
            )[h]
            n = 20 + 2 * k + h
            chunk.sum1[k, h] = go(
                remote(src, chunk.first.at[h, k], chunk.send.at[n], chunk.recv.at[n], near)
            )

    def sum2(chunk, k):
        for h, _, other, half in both_halves(chunk):
            chunk.sum1[k, h].wait_recv()
            row, column, there = ((1 - y, x, 1 - y), (y, 1 - x, 1 - x))[h]
            total = f32(partial[blocks[k], row, column, :, half]) + f32(chunk.first[h, k, there])
            partial[blocks[k], row, column, :, half] = total.astype(bf16)
            n = 28 + 2 * k + h
            chunk.sum2[k, h] = go(
                remote(
                    partial.at[blocks[k], row, column, :, half], chunk.second.at[h, k],
                    chunk.send.at[n], chunk.recv.at[n], other,
                )
            )

    def own_total(chunk, k, h):
        mine = f32(partial[blocks[k], y, x, :, chunk.halves[h]])
        return mine + f32(chunk.first[h, k, (y, x)[h]]) + f32(chunk.second[h, k])

    def square_total(chunk, k):
        for h in range(2):
            chunk.sum2[k, h].wait_recv()
            partial[blocks[k], y, x, :, chunk.halves[h]] = own_total(chunk, k, h).astype(bf16)

    def term(chunk, k):
        if chunk.kind == "z":
            return partial.at[blocks[k], y, x, :, chunk.cols]
        return partial.at[blocks[k], :, :, :, chunk.cols]

    def arrived(chunk, slot):
        ref = chunk.along.at[slot]
        remote(ref, ref, chunk.send.at[41], chunk.recv.at[41 + slot], inner_peer).wait_recv()

    def add_term(chunk, k, slots):
        if chunk.kind == "z":
            total = f32(partial[blocks[k], y, x, :, chunk.cols])
            for slot in slots:
                total = total + f32(chunk.along[slot])
            partial[blocks[k], y, x, :, chunk.cols] = total.astype(bf16)
            return

        wide = 256

        def step(i, _):
            here = pl.ds(pl.multiple_of(i * wide, wide), wide)
            cols = pl.ds(pl.multiple_of(chunk.at + i * wide, wide), wide)
            total = f32(partial[blocks[k], :, :, :, cols])
            for slot in slots:
                total = total + f32(chunk.along[slot, :, :, :, here])
            partial[blocks[k], :, :, :, cols] = total.astype(bf16)
            return 0

        lax.fori_loop(0, chunk.size // wide, step, 0)

    def sum_z(chunk, k):
        @pl.when(is_mid)
        def _():
            arrived(chunk, k)
            add_term(chunk, k, (k,))

        slot = (None, 4 * mid, end, 2 + end)[k]
        to = along(end * inner + mid * outer) if k == 2 else inner_peer
        ref = term(chunk, k)
        go(remote(ref, chunk.along.at[slot], chunk.send.at[41 + k], chunk.recv.at[41 + slot], to))

    def line_total(chunk):
        arrived(chunk, 0)

        @pl.when(is_mid)
        def _():
            arrived(chunk, 4)
            add_term(chunk, 0, (0, 4))

        @pl.when(end == 1)
        def _():
            add_term(chunk, 0, (0,))

    def finish_z(chunk):
        arrived(chunk, 0)
        size = chunk.size // 2

        @pl.when(is_mid)
        def _():
            arrived(chunk, 4)

        for h in range(2):
            chunk.sum2[0, h].wait_recv()
            here = pl.ds(h * size, size)
            total = own_total(chunk, 0, h) + f32(chunk.along[0, :, here])

            @pl.when(is_mid)
            def _():
                final[:, chunk.halves[h]] = (total + f32(chunk.along[4, :, here])).astype(bf16)

            @pl.when(end == 1)
            def _():
                final[:, chunk.halves[h]] = total.astype(bf16)

    def finish_x(chunk):
        for h in range(2):
            chunk.sum2[0, h].wait_recv()
            final[:, chunk.halves[h]] = own_total(chunk, 0, h).astype(bf16)

    graded = [0, 0]

    def hidden_step(step, _):
        cols = pl.ds(pl.multiple_of(step * 128, 128), 128)
        g = f32(gate[:, cols])
        u = f32(up[:, cols])
        value = g * jax.nn.sigmoid(g) * u
        hidden[:, cols] = value.astype(bf16)
        hidden_t[d, cols, :] = value.T.astype(bf16)
        return 0

    def forward(chunk, i):
        base = chunk.at + i * STEP
        cols = pl.ds(base, STEP)
        for b in range(ff // BLOCK):
            rows = pl.ds(b * BLOCK, BLOCK)
            for c in range(STEP // BLOCK):
                at = pl.ds(base + c * BLOCK, BLOCK)
                keep = mask_ref[b, chunk.at // BLOCK + i * (STEP // BLOCK) + c]
                keep = jnp.full((BLOCK, BLOCK), keep.astype(jnp.float32)).astype(bf16)
                weight[rows, at] = weight[rows, at] * keep
        part = jnp.dot(hidden[...], weight[:, cols], preferred_element_type=jnp.float32)
        partial[:, :, :, :, cols] = part.astype(bf16).reshape(partial.shape[:4] + (STEP,))

    def hidden_grad(chunk, part):
        begin, close = graded[part] == 0, graded[part] == len(CHUNKS) - 1
        graded[part] += 1
        wide = 256

        def step(i, _):
            rows = pl.ds(pl.multiple_of(i * wide, wide), wide)
            back = lax.dot_general(
                cot[d, :, :, :, :, chunk.cols].reshape(tokens, chunk.size),
                weight[rows, chunk.cols],
                (((1,), (1,)), ((), ())),
                preferred_element_type=jnp.float32,
            )
            if not begin:
                back = back + acc[:, rows]
            if not close:
                acc[:, rows] = back
                return 0
            g = f32(gate[:, rows])
            u = f32(up[:, rows])
            s = jax.nn.sigmoid(g)
            gate_grad[:, rows] = (back * u * s * (1.0 + g * (1.0 - s))).astype(bf16)
            up_grad[:, rows] = (back * (g * s)).astype(bf16)
            return 0

        count = ff // wide // 2
        lax.fori_loop(part * count, (part + 1) * count, step, 0)

    def weight_step(chunk, i):
        base = chunk.at + i * STEP
        cols = pl.ds(base, STEP)
        total = jnp.zeros((ff, STEP), jnp.float32)
        for core in range(2):
            total = total + jnp.dot(
                hidden_t[core],
                cot[core, :, :, :, :, cols].reshape(tokens, STEP),
                preferred_element_type=jnp.float32,
            )
        for b in range(ff // BLOCK):
            for c in range(STEP // BLOCK):
                keep = mask_ref[b, chunk.at // BLOCK + i * (STEP // BLOCK) + c]
                keep = keep.astype(jnp.float32) * scale
                block = total[b * BLOCK : (b + 1) * BLOCK, c * BLOCK : (c + 1) * BLOCK]
                at = pl.ds(base + c * BLOCK, BLOCK)
                weight_grad[pl.ds(b * BLOCK, BLOCK), at] = (block * keep).astype(bf16)

    def do_loads():
        loads[0].wait()
        loads[1].wait()

    def do_hidden():
        lax.fori_loop(0, ff // 128, hidden_step, 0)
        hidden_core.start()

    def do_forward(c, i):
        if i == 0:
            weight_loads[c].wait()
        forward(chunks[c], i)

    def do_weight(c, i):
        if i == 0:
            for k in range(4):
                chunks[c].core[k].wait_recv()
        weight_step(chunks[c], i)

    actions = {
        "loads": do_loads,
        "hidden": do_hidden,
        "own": lambda: loads[2].wait(),
        "hcore": lambda: hidden_core.wait_recv(),
        "fwd": do_forward,
        "wg": do_weight,
        "hg": lambda c, part: hidden_grad(chunks[c], part),
        "gather": lambda c: gather_z(chunks[c]),
        "pass": lambda c, k: pass_z(chunks[c], k),
        "hop1": lambda c, k: hop1(chunks[c], k),
        "hop2": lambda c, k: hop2(chunks[c], k),
        "square": lambda c, k: square(chunks[c], k),
        "core": lambda c, k: to_core(chunks[c], k),
        "sum1": lambda c, k: sum1(chunks[c], k),
        "sum2": lambda c, k: sum2(chunks[c], k),
        "total": lambda c, k: square_total(chunks[c], k),
        "sumz": lambda c, k: sum_z(chunks[c], k),
        "line": lambda c: line_total(chunks[c]),
        "endz": lambda c: finish_z(chunks[c]),
        "endx": lambda c: finish_x(chunks[c]),
    }
    for name, *args in PLAN:
        actions[name](*args)

    for copy in sent:
        copy.wait_send()

    @pl.when(is_mid)
    def _():
        for copy in sent_mid:
            copy.wait_send()

    hidden_core.wait_send()


def keep_in_hbm(array):
    return pltpu.with_memory_space_constraint(array, pltpu.HBM)


def chunk_scratch(rows, width):
    dma = pltpu.SemaphoreType.DMA
    bf16 = jnp.bfloat16
    scratch = []
    for (kind, _), (_, size) in zip(CHUNKS, chunk_columns(width)):
        levels = 4 if kind == "z" else 1
        held = (rows,) if kind == "z" else (2, 2, rows)
        scratch += [
            pltpu.VMEM((2, levels, 2, rows, size // 2), bf16),
            pltpu.VMEM((2, levels, rows, size // 2), bf16),
            pltpu.VMEM((5,) + held + (size,), bf16),
            dma((46,)),
            dma((46,)),
        ]
    return scratch


def fused(gate_pre, up_pre, down_weight, block_mask, out_grad):
    tokens, ff = gate_pre.shape
    rows, width = out_grad.shape
    scale = 1.0 / math.sqrt(tokens * 2)
    hbm = pl.BlockSpec(memory_space=pl.ANY)
    bf16 = jnp.bfloat16
    dma = pltpu.SemaphoreType.DMA
    results = pl.pallas_call(
        functools.partial(fused_kernel, scale),
        out_shape=(
            pltpu.VMEM((rows, width), bf16),
            pltpu.VMEM((tokens, ff), bf16),
            pltpu.VMEM((tokens, ff), bf16),
            pltpu.VMEM((ff, width), bf16),
        ),
        in_specs=[hbm, hbm, hbm, pl.BlockSpec(memory_space=pltpu.SMEM), hbm],
        out_specs=(pl.BlockSpec(memory_space=pltpu.VMEM),) * 4,
        scratch_shapes=[
            pltpu.VMEM((tokens, ff), bf16),
            pltpu.VMEM((tokens, ff), bf16),
            pltpu.VMEM((ff, width), bf16),
            pltpu.VMEM((2, 4, 2, 2, rows, width), bf16),
            pltpu.VMEM((tokens, ff), bf16),
            pltpu.VMEM((2, ff, tokens), bf16),
            pltpu.VMEM((4, 2, 2, rows, width), bf16),
            pltpu.VMEM((tokens, ff), jnp.float32),
            dma((3,)),
            dma((len(CHUNKS),)),
            dma((1,)),
            dma((1,)),
        ]
        + chunk_scratch(rows, width),
        compiler_params=pltpu.CompilerParams(
            collective_id=0, has_side_effects=True, vmem_limit_bytes=50 * 2**20
        ),
        cost_estimate=pl.CostEstimate(
            flops=8 * tokens * ff * width, bytes_accessed=40 * 2**20, transcendentals=2 * tokens * ff
        ),
    )(*(keep_in_hbm(a) for a in (gate_pre, up_pre, down_weight)), block_mask, keep_in_hbm(out_grad))
    return hand_on(results)


def hand_on_kernel(arrays, *refs):
    srcs, dsts, store_sem = refs[:arrays], refs[arrays : 2 * arrays], refs[2 * arrays]
    stores = [
        pltpu.make_async_copy(src, dst, store_sem.at[n])
        for n, (src, dst) in enumerate(zip(srcs, dsts))
    ]
    for store in stores:
        store.start()
    for store in stores:
        store.wait()


def hand_on(arrays):
    return pl.pallas_call(
        functools.partial(hand_on_kernel, len(arrays)),
        out_shape=tuple(jax.ShapeDtypeStruct(a.shape, a.dtype) for a in arrays),
        in_specs=[pl.BlockSpec(memory_space=pltpu.VMEM)] * len(arrays),
        out_specs=(pl.BlockSpec(memory_space=pl.ANY),) * len(arrays),
        scratch_shapes=[pltpu.SemaphoreType.DMA((len(arrays),))],
        compiler_params=pltpu.CompilerParams(vmem_limit_bytes=2 * 2**20),
    )(*(pltpu.with_memory_space_constraint(a, pltpu.VMEM) for a in arrays))


def local(gate_pre, up_pre, down_weight, block_mask, out_grad):
    blk_rows, blk_cols = block_mask.shape
    ff_local, width = down_weight.shape
    masked = (
        down_weight.reshape(blk_rows, 128, blk_cols, 128)
        * block_mask.astype(jnp.bfloat16)[:, None, :, None]
    ).reshape(ff_local, width)
    gate_val = gate_pre.astype(jnp.float32)
    up_val = up_pre.astype(jnp.float32)
    sigmoid_gate = jax.nn.sigmoid(gate_val)
    silu_gate = gate_val * sigmoid_gate
    hidden = (silu_gate * up_val).astype(jnp.bfloat16)
    layer_out = lax.psum_scatter(
        jnp.dot(hidden, masked, preferred_element_type=jnp.float32),
        "tensor",
        scatter_dimension=0,
        tiled=True,
    ).astype(jnp.bfloat16)
    cot_rows = lax.all_gather(out_grad, "tensor", axis=0, tiled=True)
    hidden_grad = lax.dot_general(
        cot_rows, masked, (((1,), (1,)), ((), ())), preferred_element_type=jnp.float32
    )
    gate_grad = (
        hidden_grad * up_val * sigmoid_gate * (1.0 + gate_val * (1.0 - sigmoid_gate))
    ).astype(jnp.bfloat16)
    up_grad = (hidden_grad * silu_gate).astype(jnp.bfloat16)
    tokens_all = out_grad.shape[0] * lax.axis_size("tensor") * lax.axis_size("dp")
    grad_scale = 1.0 / math.sqrt(tokens_all)
    partial_grad = (
        lax.dot_general(
            hidden, cot_rows, (((0,), (0,)), ((), ())), preferred_element_type=jnp.float32
        )
        * grad_scale
    )
    blocked = (
        partial_grad.reshape(blk_rows, 128, blk_cols, 128)
        * block_mask.astype(jnp.float32)[:, None, :, None]
    )
    summed = lax.psum(blocked.reshape(ff_local, width), "dp")
    weight_grad = summed.astype(jnp.bfloat16)
    return (layer_out, gate_grad, up_grad, weight_grad)


def solution(mesh):
    grouped = mesh.shape["dp"] == 2 and mesh.shape["tensor"] == 16
    return jax.shard_map(
        fused if grouped else local,
        mesh=mesh,
        in_specs=(
            P("dp", "tensor"),
            P("dp", "tensor"),
            P("tensor", None),
            P("tensor", None),
            P(("dp", "tensor"), None),
        ),
        out_specs=(
            P(("dp", "tensor"), None),
            P("dp", "tensor"),
            P("dp", "tensor"),
            P("tensor", None),
        ),
        check_vma=False,
    )
```

time: 98.7 us -> 82.6 us (0.84)
  Pallas kernels: 97.8 us -> 81.6 us
    pallas_call x1, Pallas kernels: 93.6 us -> 77.4 us  [fused(): pl.pallas_call(functools.partial(fused_kernel, scale), out_shape=(pltpu.V...]
where the time goes in v2:
time: 82.6 us; the launch traced here: 82.4 us
  Pallas kernels  81.6 us (99%)
    pallas_call x1, Pallas kernels, fused(): pl.pallas_call(functools.partial(fused_kernel, scale), out_shape=(pltpu.V...  77.4 us
    pallas_call x1, Pallas kernels, hand_on(): pl.pallas_call(functools.partial(hand_on_kernel, len(arrays)), out_shape=...  4.21 us

profile of v2, /device:TPU:0, one launch (start us, length us, event | category | flops | bytes accessed | tf_op | source)
XLA Modules:
  0.0 82.4 jit_solution(12397737453778163694)
XLA Ops:
  0.6 77.4 %shard_map.84 = (bf16[32,4096]{1,0:T(8,128)(2,1)S(1)}, bf16[512,1024]{1,0:T(8,128)(2,1)S(1)}, bf16[512,1024]{1,0:T(8,128)(2,1)S(1)}, bf16[1024,4096]{1,0:T(8,128)(2,1)S(1)}) custom-call(bf16[512,1024]{1,0:T(8,128)(2,1)} %gate_hbm.1, bf16[512,1024]{1,0:T(8,128)(2,1)} %up_hbm.1, bf16[1024,4096]{1,0:T(8,128)(2,1)} %weight_hbm.1, s32[8,32]{1,0:T(8,128)} %mask_ref.1, ...), custom_call_target="tpu_custom_call" | custom-call | flops 17179869184 | bytes 41943040 | tf_op jit(solution)/shard_map/pallas_call | solution.py:493
  78.0 4.2 %shard_map.85 = (bf16[32,4096]{1,0:T(8,128)(2,1)}, bf16[512,1024]{1,0:T(8,128)(2,1)}, bf16[512,1024]{1,0:T(8,128)(2,1)}, bf16[1024,4096]{1,0:T(8,128)(2,1)}) custom-call(bf16[32,4096]{1,0:T(8,128)(2,1)S(1)} %get-tuple-element.8.refs_0_, bf16[512,1024]{1,0:T(8,128)(2,1)S(1)} %get-tuple-element.9.refs_1_, bf16[512,1024]{1,0:T(8,128)(2,1)S(1)} %get-tuple-element.10.refs_2_, ...), custom_call_target="tpu_custom_call" | custom-call | tf_op jit(solution)/shard_map/pallas_call | solution.py:541

commit v3 on v2

--- a/solution.py
+++ b/solution.py
@@ -10,47 +10,46 @@
 
 BLOCK = 128
 STEP = 512
-CHUNKS = (("z", 1), ("z", 2), ("z", 2), ("x", 1), ("x", 1), ("x", 1))
+CHUNKS = (("z", 2), ("z", 1), ("z", 2), ("x", 1), ("x", 1), ("x", 1))
 CHUNK_SCRATCH = 5
 
 
-FORWARD = (0, 1, 5, 4, 3, 2)
+FORWARD = (0, 1, 2, 3, 4, 5)
 PLAN = (
-    ("gather", 1), ("hop1", 5, 0), ("hop1", 4, 0), ("hop1", 3, 0), ("gather", 0), ("own",),
-    ("hop1", 1, 0), ("hop1", 2, 0), ("hop2", 5, 0), ("hop2", 4, 0), ("loads",), ("hop1", 0, 0),
-    ("hop2", 3, 0), ("pass", 1, 0), ("pass", 1, 1), ("gather", 2), ("hop1", 1, 1), ("hop1", 1, 2),
-    ("hop2", 1, 0), ("hidden",), ("hop2", 2, 0), ("square", 5, 0), ("core", 5, 0), ("pass", 1, 2),
-    ("pass", 0, 0), ("gather", 5), ("fwd", 0, 0), ("sum1", 0, 3), ("pass", 2, 0), ("pass", 0, 1),
-    ("hop1", 1, 3), ("hop1", 0, 1), ("fwd", 1, 0), ("square", 4, 0), ("gather", 4),
-    ("hop2", 1, 2), ("hop1", 0, 2), ("hop2", 1, 1), ("fwd", 1, 1), ("hop1", 2, 1),
-    ("square", 2, 0), ("square", 1, 0), ("square", 3, 0), ("hop2", 1, 3), ("core", 4, 0),
-    ("gather", 3), ("sum1", 0, 1), ("pass", 5, 0), ("core", 2, 0), ("fwd", 5, 0), ("fwd", 4, 0),
-    ("sum1", 1, 2), ("hop2", 0, 2), ("hop2", 0, 0), ("sum2", 0, 3), ("core", 1, 0),
-    ("square", 1, 2), ("core", 1, 2), ("pass", 4, 0), ("core", 3, 0), ("core", 5, 1),
-    ("square", 1, 1), ("hop2", 0, 1), ("sum1", 0, 0), ("core", 4, 1), ("pass", 2, 1),
-    ("hop1", 2, 2), ("sumz", 5, 3), ("hop2", 2, 1), ("sum1", 0, 2), ("fwd", 3, 0),
-    ("square", 1, 3), ("core", 1, 3), ("core", 1, 1), ("hg", 1, 0), ("sum2", 0, 1),
-    ("pass", 3, 0), ("sumz", 3, 3), ("fwd", 2, 0), ("sum1", 1, 1), ("square", 0, 2),
-    ("core", 3, 1), ("fwd", 2, 1), ("pass", 5, 1), ("sum2", 1, 2), ("sumz", 4, 3), ("pass", 2, 2),
-    ("pass", 3, 1), ("core", 0, 2), ("sumz", 5, 2), ("total", 0, 3), ("hop1", 2, 3), ("hg", 1, 1),
-    ("sum1", 1, 0), ("hcore",), ("wg", 1, 0), ("hop2", 2, 2), ("core", 3, 2), ("total", 1, 2),
-    ("pass", 4, 1), ("sum2", 1, 1), ("hop2", 2, 3), ("sum2", 0, 2), ("core", 5, 2),
-    ("sum1", 2, 1), ("sum1", 2, 2), ("sum1", 2, 3), ("core", 4, 2), ("square", 2, 1),
-    ("square", 0, 0), ("pass", 5, 2), ("sumz", 3, 2), ("core", 2, 1), ("core", 0, 0),
-    ("sum2", 0, 0), ("hg", 5, 0), ("core", 5, 3), ("sum1", 1, 3), ("wg", 1, 1), ("sum2", 1, 0),
-    ("sum1", 2, 0), ("sumz", 4, 2), ("sumz", 5, 1), ("square", 2, 2), ("wg", 5, 0),
-    ("core", 2, 2), ("total", 0, 1), ("square", 0, 1), ("square", 2, 3), ("core", 2, 3),
-    ("hg", 2, 0), ("hg", 2, 1), ("wg", 2, 0), ("pass", 0, 2), ("hop1", 0, 3), ("sumz", 3, 1),
-    ("sum2", 2, 2), ("hg", 5, 1), ("core", 0, 1), ("sum2", 2, 3), ("pass", 4, 2), ("sum2", 2, 1),
-    ("total", 1, 1), ("hg", 4, 0), ("sum2", 1, 3), ("hg", 4, 1), ("sumz", 4, 1), ("wg", 2, 1),
-    ("total", 0, 2), ("hop2", 0, 3), ("pass", 3, 2), ("line", 3), ("line", 5), ("sum1", 5, 0),
-    ("sum1", 3, 0), ("total", 2, 3), ("line", 4), ("sum1", 4, 0), ("total", 2, 1),
-    ("total", 1, 3), ("sum2", 2, 0), ("total", 2, 2), ("core", 4, 3), ("sumz", 0, 3),
-    ("hg", 3, 0), ("core", 3, 3), ("sumz", 2, 3), ("square", 0, 3), ("hg", 0, 0), ("core", 0, 3),
-    ("sumz", 1, 3), ("sum2", 4, 0), ("sumz", 0, 2), ("sum2", 3, 0), ("sum2", 5, 0), ("hg", 3, 1),
-    ("sumz", 2, 2), ("sumz", 0, 1), ("hg", 0, 1), ("sumz", 1, 2), ("sumz", 2, 1), ("endx", 4),
-    ("wg", 4, 0), ("sumz", 1, 1), ("endx", 5), ("wg", 3, 0), ("endx", 3), ("endz", 0),
-    ("wg", 0, 0), ("endz", 2), ("endz", 1),
+    ("hop1", 4, 0), ("gather", 1), ("gather", 2), ("hop1", 5, 0), ("own",), ("hop1", 3, 0),
+    ("hop1", 2, 0), ("hop1", 1, 0), ("hop2", 4, 0), ("gather", 0), ("hop1", 0, 0), ("pass", 1, 0),
+    ("hop2", 5, 0), ("loads",), ("hidden",), ("pass", 2, 0), ("hop2", 3, 0), ("hop2", 1, 0),
+    ("hop1", 1, 1), ("square", 4, 0), ("gather", 4), ("fwd", 0, 0), ("hop2", 0, 0), ("fwd", 1, 0),
+    ("square", 5, 0), ("hop1", 2, 1), ("gather", 5), ("fwd", 2, 0), ("fwd", 0, 1), ("pass", 1, 1),
+    ("core", 4, 0), ("pass", 0, 0), ("square", 3, 0), ("hop1", 1, 2), ("sum1", 1, 1),
+    ("gather", 3), ("sum1", 0, 1), ("pass", 2, 1), ("fwd", 2, 1), ("sum1", 1, 0), ("fwd", 3, 0),
+    ("hop2", 2, 0), ("hop1", 2, 2), ("sum1", 1, 3), ("pass", 4, 0), ("fwd", 4, 0), ("core", 5, 0),
+    ("sum1", 2, 2), ("core", 4, 1), ("sum1", 0, 3), ("sum1", 0, 2), ("sumz", 4, 3),
+    ("pass", 5, 0), ("hop2", 1, 1), ("hop2", 2, 1), ("fwd", 5, 0), ("sumz", 5, 3), ("pass", 3, 0),
+    ("hop2", 1, 2), ("sum1", 2, 3), ("sum1", 1, 2), ("sumz", 3, 3), ("pass", 2, 2),
+    ("hop1", 2, 3), ("core", 3, 0), ("square", 1, 2), ("pass", 0, 1), ("sum2", 0, 2),
+    ("square", 0, 0), ("pass", 1, 2), ("sumz", 4, 2), ("square", 1, 1), ("pass", 3, 1),
+    ("hop1", 1, 3), ("hop2", 2, 2), ("hop2", 2, 3), ("pass", 5, 1), ("square", 2, 0),
+    ("sum2", 1, 1), ("sumz", 5, 2), ("sum2", 2, 2), ("hop2", 1, 3), ("pass", 4, 1),
+    ("core", 4, 2), ("square", 2, 1), ("core", 5, 2), ("hcore",), ("core", 1, 1), ("hop1", 0, 1),
+    ("square", 1, 0), ("core", 3, 1), ("sum2", 0, 3), ("sum2", 1, 3), ("sum2", 1, 2),
+    ("sum1", 2, 1), ("square", 2, 2), ("core", 5, 1), ("hop1", 0, 2), ("sum2", 0, 1),
+    ("sum2", 1, 0), ("sum2", 2, 3), ("sumz", 3, 2), ("square", 2, 3), ("total", 0, 2),
+    ("hg", 2, 0), ("total", 1, 1), ("core", 1, 2), ("hg", 2, 1), ("core", 2, 2), ("core", 2, 1),
+    ("square", 1, 3), ("hg", 1, 0), ("total", 2, 2), ("sumz", 4, 1), ("core", 2, 0),
+    ("sum1", 2, 0), ("core", 2, 3), ("hop2", 0, 1), ("core", 1, 0), ("pass", 3, 2), ("hg", 3, 0),
+    ("core", 1, 3), ("core", 3, 3), ("core", 0, 0), ("total", 0, 3), ("core", 3, 2), ("hg", 1, 1),
+    ("total", 1, 2), ("total", 1, 3), ("pass", 0, 2), ("sumz", 5, 1), ("hop1", 0, 3),
+    ("hg", 3, 1), ("wg", 2, 0), ("sum2", 2, 1), ("pass", 5, 2), ("sumz", 3, 1), ("hop2", 0, 2),
+    ("wg", 3, 0), ("hg", 5, 0), ("sum1", 0, 0), ("total", 2, 3), ("hg", 5, 1), ("pass", 4, 2),
+    ("square", 0, 1), ("sumz", 1, 3), ("core", 4, 3), ("line", 3), ("total", 0, 1),
+    ("hop2", 0, 3), ("line", 5), ("line", 4), ("sum1", 5, 0), ("sumz", 0, 3), ("sum1", 3, 0),
+    ("core", 5, 3), ("sum1", 4, 0), ("wg", 4, 0), ("sum2", 2, 0), ("core", 0, 1), ("total", 2, 1),
+    ("sumz", 2, 3), ("wg", 5, 0), ("sumz", 1, 2), ("hg", 4, 0), ("sum2", 0, 0), ("square", 0, 2),
+    ("core", 0, 2), ("sumz", 1, 1), ("hg", 4, 1), ("sumz", 0, 2), ("sum2", 5, 0),
+    ("square", 0, 3), ("core", 0, 3), ("wg", 1, 0), ("sum2", 4, 0), ("sum2", 3, 0),
+    ("sumz", 2, 2), ("sumz", 0, 1), ("wg", 0, 0), ("sumz", 2, 1), ("hg", 0, 0), ("endx", 5),
+    ("hg", 0, 1), ("endz", 1), ("endx", 3), ("endx", 4), ("endz", 0), ("endz", 2),
 )
 
 
@@ -219,7 +218,9 @@
             chunk.hop2[k, h].wait_recv()
 
     def to_core(chunk, k):
-        ref = cot.at[d, blocks[k], :, :, :, chunk.cols]
+        size = chunk.size // 2
+        cols = pl.ds(pl.multiple_of(chunk.at + (1 - d) * size, 256), size)
+        ref = cot.at[d, blocks[k], :, :, :, cols]
         chunk.core[k] = go(
             remote(ref, ref, chunk.send.at[16 + k], chunk.recv.at[16 + k], core_peer)
         )
@@ -352,19 +353,23 @@
         base = chunk.at + i * STEP
         cols = pl.ds(base, STEP)
         for b in range(ff // BLOCK):
-            rows = pl.ds(b * BLOCK, BLOCK)
-            for c in range(STEP // BLOCK):
-                at = pl.ds(base + c * BLOCK, BLOCK)
-                keep = mask_ref[b, chunk.at // BLOCK + i * (STEP // BLOCK) + c]
-                keep = jnp.full((BLOCK, BLOCK), keep.astype(jnp.float32)).astype(bf16)
-                weight[rows, at] = weight[rows, at] * keep
+            keep = jnp.concatenate(
+                [
+                    jnp.full((16, BLOCK), f32(mask_ref[b, base // BLOCK + c])).astype(bf16)
+                    for c in range(STEP // BLOCK)
+                ],
+                axis=1,
+            )
+            for r in range(BLOCK // 16):
+                rows = pl.ds(b * BLOCK + r * 16, 16)
+                weight[rows, cols] = weight[rows, cols] * keep
         part = jnp.dot(hidden[...], weight[:, cols], preferred_element_type=jnp.float32)
         partial[:, :, :, :, cols] = part.astype(bf16).reshape(partial.shape[:4] + (STEP,))
 
     def hidden_grad(chunk, part):
         begin, close = graded[part] == 0, graded[part] == len(CHUNKS) - 1
         graded[part] += 1
-        wide = 256
+        wide = 512
 
         def step(i, _):
             rows = pl.ds(pl.multiple_of(i * wide, wide), wide)
@@ -389,23 +394,29 @@
         count = ff // wide // 2
         lax.fori_loop(part * count, (part + 1) * count, step, 0)
 
-    def weight_step(chunk, i):
-        base = chunk.at + i * STEP
-        cols = pl.ds(base, STEP)
-        total = jnp.zeros((ff, STEP), jnp.float32)
+    def weight_half(chunk):
+        size = chunk.size // 2
+        base = pl.multiple_of(chunk.at + d * size, 256)
+        cols = pl.ds(base, size)
+        total = jnp.zeros((ff, size), jnp.float32)
         for core in range(2):
             total = total + jnp.dot(
                 hidden_t[core],
-                cot[core, :, :, :, :, cols].reshape(tokens, STEP),
+                cot[core, :, :, :, :, cols].reshape(tokens, size),
                 preferred_element_type=jnp.float32,
             )
         for b in range(ff // BLOCK):
-            for c in range(STEP // BLOCK):
-                keep = mask_ref[b, chunk.at // BLOCK + i * (STEP // BLOCK) + c]
-                keep = keep.astype(jnp.float32) * scale
+            for c in range(size // BLOCK):
+                keep = f32(mask_ref[b, chunk.at // BLOCK + d * (size // BLOCK) + c]) * scale
                 block = total[b * BLOCK : (b + 1) * BLOCK, c * BLOCK : (c + 1) * BLOCK]
-                at = pl.ds(base + c * BLOCK, BLOCK)
+                at = pl.ds(pl.multiple_of(base + c * BLOCK, BLOCK), BLOCK)
                 weight_grad[pl.ds(b * BLOCK, BLOCK), at] = (block * keep).astype(bf16)
+        chunk.half = go(
+            remote(
+                weight_grad.at[:, cols], weight_grad.at[:, cols], chunk.send.at[46],
+                chunk.recv.at[46], core_peer,
+            )
+        )
 
     def do_loads():
         loads[0].wait()
@@ -420,11 +431,10 @@
             weight_loads[c].wait()
         forward(chunks[c], i)
 
-    def do_weight(c, i):
-        if i == 0:
-            for k in range(4):
-                chunks[c].core[k].wait_recv()
-        weight_step(chunks[c], i)
+    def do_weight(c, _):
+        for k in range(4):
+            chunks[c].core[k].wait_recv()
+        weight_half(chunks[c])
 
     actions = {
         "loads": do_loads,
@@ -451,6 +461,8 @@
     for name, *args in PLAN:
         actions[name](*args)
 
+    for chunk in chunks:
+        chunk.half.wait_recv()
     for copy in sent:
         copy.wait_send()
 
@@ -477,8 +489,8 @@
             pltpu.VMEM((2, levels, 2, rows, size // 2), bf16),
             pltpu.VMEM((2, levels, rows, size // 2), bf16),
             pltpu.VMEM((5,) + held + (size,), bf16),
-            dma((46,)),
-            dma((46,)),
+            dma((47,)),
+            dma((47,)),
         ]
     return scratch
 

time: 82.6 us -> 76.2 us (0.923)
  Pallas kernels: 81.6 us -> 74.9 us
    pallas_call x1, Pallas kernels: 77.4 us -> 70.7 us  [fused(): pl.pallas_call(functools.partial(fused_kernel, scale), out_shape=(pltpu.V...]
where the time goes in v3:
time: 76.2 us; the launch traced here: 75.7 us
  Pallas kernels  74.9 us (98%)
  between operations  0.8 us (1%)
    pallas_call x1, Pallas kernels, fused(): pl.pallas_call(functools.partial(fused_kernel, scale), out_shape=(pltpu.V...  70.7 us
    pallas_call x1, Pallas kernels, hand_on(): pl.pallas_call(functools.partial(hand_on_kernel, len(arrays)), out_shape=...  4.21 us

profile of v3, /device:TPU:0, one launch (start us, length us, event | category | flops | bytes accessed | tf_op | source)
XLA Modules:
  0.0 75.7 jit_solution(17047293813828439648)
XLA Ops:
  0.6 70.7 %shard_map.84 = (bf16[32,4096]{1,0:T(8,128)(2,1)S(1)}, bf16[512,1024]{1,0:T(8,128)(2,1)S(1)}, bf16[512,1024]{1,0:T(8,128)(2,1)S(1)}, bf16[1024,4096]{1,0:T(8,128)(2,1)S(1)}) custom-call(bf16[512,1024]{1,0:T(8,128)(2,1)} %gate_hbm.1, bf16[512,1024]{1,0:T(8,128)(2,1)} %up_hbm.1, bf16[1024,4096]{1,0:T(8,128)(2,1)} %weight_hbm.1, s32[8,32]{1,0:T(8,128)} %mask_ref.1, ...), custom_call_target="tpu_custom_call" | custom-call | flops 17179869184 | bytes 41943040 | tf_op jit(solution)/shard_map/pallas_call | solution.py:505
  71.3 4.2 %shard_map.85 = (bf16[32,4096]{1,0:T(8,128)(2,1)}, bf16[512,1024]{1,0:T(8,128)(2,1)}, bf16[512,1024]{1,0:T(8,128)(2,1)}, bf16[1024,4096]{1,0:T(8,128)(2,1)}) custom-call(bf16[32,4096]{1,0:T(8,128)(2,1)S(1)} %get-tuple-element.8.refs_0_, bf16[512,1024]{1,0:T(8,128)(2,1)S(1)} %get-tuple-element.9.refs_1_, bf16[512,1024]{1,0:T(8,128)(2,1)S(1)} %get-tuple-element.10.refs_2_, ...), custom_call_target="tpu_custom_call" | custom-call | tf_op jit(solution)/shard_map/pallas_call | solution.py:553

commit v4 on v2

v4 whole, which is shorter than its diff:
```python
import functools
import math

import jax
import jax.numpy as jnp
from jax import lax
from jax.experimental import pallas as pl
from jax.experimental.pallas import tpu as pltpu
from jax.sharding import PartitionSpec as P

BLOCK = 128
STEP = 512
CHUNKS = (("z", 1), ("z", 2), ("z", 2), ("x", 1), ("x", 1), ("x", 1))
CHUNK_SCRATCH = 5


FORWARD = (1, 4, 0, 5, 2, 3)
MID_PLAN = (
    ("hop1", 3, 0), ("hop1", 4, 0), ("gather", 0), ("gather", 2), ("hop1", 5, 0), ("hop1", 1, 0),
    ("gather", 1), ("hop1", 0, 0), ("hop1", 2, 0), ("own",), ("hop2", 3, 0), ("pass", 0, 0),
    ("pass", 0, 1), ("hop1", 0, 1), ("hop2", 5, 0), ("hop2", 1, 0), ("pass", 2, 0),
    ("pass", 1, 1), ("hop1", 0, 2), ("pass", 1, 0), ("hop1", 1, 1), ("hop2", 4, 0),
    ("square", 3, 0), ("hop1", 2, 1), ("pass", 0, 2), ("pass", 2, 1), ("hop1", 2, 2), ("loads",),
    ("gather", 3), ("hidden",), ("square", 5, 0), ("pass", 1, 2), ("square", 1, 0),
    ("hop2", 0, 1), ("hop2", 2, 0), ("fwd", 1, 0), ("gather", 5), ("hop1", 0, 3), ("hop2", 0, 0),
    ("pass", 2, 2), ("core", 5, 0), ("fwd", 4, 0), ("fwd", 0, 0), ("hop1", 1, 2), ("fwd", 5, 0),
    ("square", 4, 0), ("pass", 3, 1), ("hop2", 2, 2), ("hcore",), ("hop1", 2, 3), ("core", 4, 0),
    ("pass", 3, 0), ("fwd", 2, 0), ("fwd", 2, 1), ("hop2", 1, 1), ("hop1", 1, 3),
    ("square", 0, 0), ("pass", 5, 0), ("pass", 5, 1), ("fwd", 1, 1), ("hop2", 2, 1),
    ("pass", 4, 1), ("hop2", 0, 3), ("pass", 3, 2), ("sumz", 4, 3), ("hop2", 2, 3), ("gather", 4),
    ("square", 1, 1), ("core", 3, 3), ("hop2", 1, 3), ("sum1", 0, 3), ("sum1", 2, 1),
    ("pass", 5, 2), ("square", 2, 0), ("hop2", 1, 2), ("square", 2, 3), ("hg", 5, 0),
    ("sum1", 2, 3), ("sum2", 0, 3), ("hop2", 0, 2), ("fwd", 3, 0), ("sum1", 0, 2), ("sum1", 1, 1),
    ("sumz", 3, 3), ("square", 2, 2), ("sum1", 1, 2), ("hg", 5, 1), ("sum2", 2, 1),
    ("sumz", 5, 3), ("square", 1, 3), ("core", 0, 0), ("core", 1, 0), ("square", 2, 1),
    ("square", 0, 3), ("square", 0, 1), ("hg", 2, 0), ("pass", 4, 0), ("core", 1, 3),
    ("square", 1, 2), ("sum1", 0, 1), ("total", 0, 3), ("sum1", 1, 3), ("sum1", 2, 0),
    ("core", 5, 1), ("sumz", 4, 1), ("core", 5, 3), ("hg", 1, 0), ("core", 2, 3), ("hg", 3, 0),
    ("sumz", 4, 2), ("core", 4, 1), ("sumz", 3, 1), ("square", 0, 2), ("sumz", 3, 2),
    ("hg", 2, 1), ("core", 2, 0), ("core", 2, 2), ("hg", 3, 1), ("hg", 0, 0), ("core", 2, 1),
    ("core", 0, 2), ("core", 1, 1), ("core", 1, 2), ("core", 3, 1), ("sum2", 0, 2),
    ("sumz", 5, 2), ("sum2", 2, 3), ("pass", 4, 2), ("core", 3, 0), ("hg", 4, 0), ("core", 3, 2),
    ("sumz", 5, 1), ("sum2", 1, 2), ("sum2", 1, 3), ("core", 4, 3), ("core", 4, 2),
    ("core", 0, 3), ("sum2", 0, 1), ("sumz", 0, 3), ("sum1", 2, 2), ("total", 2, 1), ("line", 4),
    ("sum1", 4, 0), ("sum1", 1, 0), ("hg", 0, 1), ("hg", 1, 1), ("sum2", 1, 1), ("wg", 2, 0),
    ("total", 1, 3), ("sumz", 1, 3), ("wg", 4, 0), ("total", 1, 2), ("total", 0, 2), ("line", 3),
    ("total", 2, 3), ("sum1", 3, 0), ("total", 0, 1), ("sum2", 2, 2), ("core", 0, 1),
    ("sumz", 2, 3), ("core", 5, 2), ("wg", 1, 0), ("sum1", 0, 0), ("line", 5), ("sum1", 5, 0),
    ("sum2", 2, 0), ("sum2", 1, 0), ("sumz", 0, 1), ("sumz", 2, 1), ("sumz", 0, 2),
    ("sum2", 4, 0), ("sumz", 1, 2), ("sum2", 3, 0), ("total", 1, 1), ("wg", 0, 0),
    ("total", 2, 2), ("sumz", 2, 2), ("sumz", 1, 1), ("wg", 3, 0), ("sum2", 0, 0), ("sum2", 5, 0),
    ("wg", 5, 0), ("hg", 4, 1), ("endz", 0), ("endz", 1), ("endz", 2), ("endx", 4), ("endx", 3),
    ("endx", 5),
)
END_PLAN = (
    ("hop1", 3, 0), ("gather", 0), ("hop1", 5, 0), ("hop1", 1, 0), ("own",), ("hop1", 0, 0),
    ("gather", 1), ("hop1", 4, 0), ("gather", 2), ("hop1", 2, 0), ("loads",), ("hidden",),
    ("hop2", 5, 0), ("hop2", 3, 0), ("fwd", 4, 0), ("hop2", 1, 0), ("sumz", 4, 3), ("hop2", 4, 0),
    ("pass", 0, 0), ("fwd", 2, 0), ("fwd", 2, 1), ("pass", 2, 0), ("sum1", 2, 3), ("fwd", 0, 0),
    ("square", 5, 0), ("pass", 1, 0), ("sum1", 0, 2), ("square", 3, 0), ("hop1", 1, 1),
    ("pass", 0, 1), ("gather", 3), ("gather", 5), ("hop1", 0, 1), ("pass", 2, 1), ("fwd", 3, 0),
    ("core", 3, 0), ("hop1", 0, 2), ("hcore",), ("square", 4, 0), ("hop2", 2, 0), ("fwd", 5, 0),
    ("hop1", 2, 2), ("gather", 4), ("pass", 1, 1), ("sum2", 0, 2), ("hop2", 1, 1), ("hop1", 1, 2),
    ("pass", 3, 0), ("pass", 0, 2), ("hop2", 0, 0), ("hop2", 0, 1), ("sum1", 0, 3),
    ("pass", 1, 2), ("hop1", 1, 3), ("sumz", 5, 3), ("sumz", 4, 2), ("sum1", 2, 2),
    ("square", 0, 1), ("hop2", 1, 2), ("sum2", 2, 3), ("square", 1, 0), ("hop2", 1, 3),
    ("sumz", 3, 3), ("square", 2, 0), ("sumz", 3, 2), ("pass", 2, 2), ("fwd", 1, 0),
    ("pass", 3, 1), ("core", 1, 0), ("hop1", 0, 3), ("sumz", 4, 1), ("fwd", 1, 1), ("pass", 5, 0),
    ("sum1", 1, 3), ("sum1", 0, 1), ("square", 1, 1), ("hop1", 2, 1), ("square", 1, 2),
    ("pass", 5, 1), ("sumz", 5, 2), ("total", 0, 2), ("core", 3, 2), ("hop2", 0, 3),
    ("hop2", 0, 2), ("sum2", 1, 3), ("square", 1, 3), ("core", 1, 2), ("sum1", 1, 2),
    ("sumz", 3, 1), ("sum2", 0, 3), ("hg", 1, 0), ("core", 5, 1), ("core", 1, 1), ("hop1", 2, 3),
    ("total", 2, 3), ("hop2", 2, 1), ("square", 0, 2), ("sum2", 2, 2), ("pass", 3, 2),
    ("core", 5, 2), ("total", 1, 3), ("hg", 3, 0), ("hg", 3, 1), ("core", 1, 3), ("sum2", 1, 2),
    ("pass", 5, 2), ("pass", 4, 0), ("hop2", 2, 2), ("hg", 5, 0), ("core", 5, 0), ("hg", 5, 1),
    ("square", 0, 0), ("sum1", 1, 1), ("sum2", 0, 1), ("total", 0, 3), ("hop2", 2, 3),
    ("core", 3, 1), ("core", 2, 0), ("sumz", 0, 3), ("square", 0, 3), ("core", 0, 3),
    ("core", 5, 3), ("core", 0, 1), ("sumz", 1, 3), ("sumz", 2, 3), ("core", 0, 2),
    ("core", 3, 3), ("sumz", 5, 1), ("wg", 1, 0), ("sum1", 2, 1), ("total", 2, 2), ("sumz", 2, 2),
    ("hg", 0, 0), ("core", 4, 1), ("sum1", 2, 0), ("square", 2, 1), ("hg", 0, 1), ("core", 0, 0),
    ("wg", 3, 0), ("wg", 5, 0), ("wg", 0, 0), ("core", 2, 1), ("sum1", 1, 0), ("square", 2, 2),
    ("total", 1, 2), ("total", 0, 1), ("sumz", 0, 2), ("line", 3), ("sum2", 1, 1), ("sum1", 0, 0),
    ("sum1", 3, 0), ("pass", 4, 1), ("square", 2, 3), ("core", 2, 2), ("core", 2, 3),
    ("sumz", 0, 1), ("line", 4), ("hg", 1, 1), ("sum2", 2, 1), ("sumz", 1, 2), ("line", 5),
    ("sum1", 5, 0), ("core", 4, 2), ("sum1", 4, 0), ("wg", 2, 0), ("hg", 2, 0), ("pass", 4, 2),
    ("sum2", 2, 0), ("core", 4, 0), ("total", 1, 1), ("sumz", 1, 1), ("core", 4, 3),
    ("sum2", 1, 0), ("hg", 4, 0), ("sum2", 3, 0), ("total", 2, 1), ("sum2", 0, 0), ("sumz", 2, 1),
    ("wg", 4, 0), ("sum2", 5, 0), ("sum2", 4, 0), ("hg", 4, 1), ("hg", 2, 1), ("endz", 1),
    ("endz", 2), ("endx", 3), ("endx", 5), ("endz", 0), ("endx", 4),
)


def remote(src, dst, send, recv, device):
    return pltpu.make_async_remote_copy(
        src_ref=src,
        dst_ref=dst,
        send_sem=send,
        recv_sem=recv,
        device_id=device,
        device_id_type=pl.DeviceIdType.MESH,
    )


def chunk_columns(width):
    unit = width // 8
    at, spans = 0, []
    for _, units in CHUNKS:
        spans.append((at, units * unit))
        at += units * unit
    return spans


def f32(value):
    return value.astype(jnp.float32)


def fused_kernel(
    scale,
    gate_hbm, up_hbm, weight_hbm, mask_ref, grad_hbm,
    final, gate_grad, up_grad, weight_grad,
    gate, up, weight, cot, hidden, hidden_t, partial, acc,
    in_sem, weight_sem, hidden_send, hidden_recv,
    *scratch,
):
    d = lax.axis_index("dp")
    t = lax.axis_index("tensor")
    x = t % 2
    y = (t // 2) % 2
    z = t // 4
    ff, width = weight.shape
    tokens = gate.shape[0]
    bf16 = jnp.bfloat16
    spans = chunk_columns(width)

    mid = ((z + 1) // 2) % 2
    end = 1 - mid
    is_mid = mid == 1
    inner = mid * (3 - z) + end * (1 + z // 3)
    outer = mid * (z - 1) * 3
    far = end * (3 - z) + mid * (2 - z) * 3
    blocks = (z, inner, end * (3 - inner) + mid * outer, far)

    def along(level):
        return {"tensor": level * 4 + y * 2 + x}

    x_peer = {"tensor": z * 4 + y * 2 + (1 - x)}
    y_peer = {"tensor": z * 4 + (1 - y) * 2 + x}
    core_peer = {"dp": 1 - d}
    inner_peer, outer_peer = along(inner), along(outer)

    loads = [
        pltpu.make_async_copy(gate_hbm, gate, in_sem.at[0]),
        pltpu.make_async_copy(up_hbm, up, in_sem.at[1]),
        pltpu.make_async_copy(grad_hbm, cot.at[d, z, y, x], in_sem.at[2]),
    ]
    weight_loads = {}
    for c, (at, size) in enumerate(spans):
        cols = pl.ds(at, size)
        weight_loads[c] = pltpu.make_async_copy(
            weight_hbm.at[:, cols], weight.at[:, cols], weight_sem.at[c]
        )
    for copy in loads:
        copy.start()
    for c in FORWARD:
        weight_loads[c].start()

    barrier = pltpu.get_barrier_semaphore()
    for peer in (x_peer, y_peer, core_peer, inner_peer):
        pl.semaphore_signal(barrier, inc=1, device_id=peer, device_id_type=pl.DeviceIdType.MESH)

    @pl.when(is_mid)
    def _():
        pl.semaphore_signal(
            barrier, inc=1, device_id=outer_peer, device_id_type=pl.DeviceIdType.MESH
        )

    pl.semaphore_wait(barrier, 4 + mid)

    def run(is_mid, plan):
        mid = int(is_mid)
        end = 1 - mid

        hidden_core = remote(
            hidden_t.at[d], hidden_t.at[d], hidden_send.at[0], hidden_recv.at[0], core_peer
        )
        sent = []

        def go(copy):
            copy.start()
            sent.append(copy)
            return copy

        class Chunk:
            pass

        def both_halves(chunk):
            return ((0, x_peer, y_peer, chunk.halves[0]), (1, y_peer, x_peer, chunk.halves[1]))

        chunks = []
        for c, (kind, _) in enumerate(CHUNKS):
            chunk = Chunk()
            at, size = spans[c]
            chunk.kind, chunk.at, chunk.size = kind, at, size
            chunk.cols = pl.ds(at, size)
            chunk.halves = (pl.ds(at, size // 2), pl.ds(at + size // 2, size // 2))
            chunk.first, chunk.second, chunk.along, chunk.send, chunk.recv = scratch[
                CHUNK_SCRATCH * c : CHUNK_SCRATCH * (c + 1)
            ]
            chunk.hop1, chunk.hop2, chunk.core, chunk.sum1, chunk.sum2 = {}, {}, {}, {}, {}
            chunks.append(chunk)


        def piece(chunk, b):
            if chunk.kind == "z":
                return cot.at[d, b, y, x, :, chunk.cols]
            return cot.at[d, b, :, :, :, chunk.cols]

        def gather_z(chunk):
            own = piece(chunk, z)
            src = grad_hbm.at[:, chunk.cols] if chunk.kind == "z" else own
            go(remote(src, own, chunk.send.at[36], chunk.recv.at[36 + end], inner_peer))

            if is_mid:
                go(remote(src, own, chunk.send.at[37], chunk.recv.at[36], outer_peer))

        def pass_z(chunk, s):
            block = piece(chunk, blocks[s + 1])
            remote(block, block, chunk.send.at[36], chunk.recv.at[36 + s], inner_peer).wait_recv()
            if not is_mid:
                return
            to, slot = ((outer_peer, 1), (inner_peer, 2), (outer_peer, 2))[s]
            copy = remote(block, block, chunk.send.at[38 + s], chunk.recv.at[36 + slot], to)

            go(copy)

        def hop1(chunk, k):
            for h, near, _, half in both_halves(chunk):
                dst = cot.at[d, blocks[k], y, x, :, half]
                src = grad_hbm.at[:, half] if k == 0 else dst
                n = 2 * k + h
                chunk.hop1[k, h] = go(remote(src, dst, chunk.send.at[n], chunk.recv.at[n], near))

        def hop2(chunk, k):
            for h in range(2):
                chunk.hop1[k, h].wait_recv()
            for h, _, other, half in both_halves(chunk):
                ref = (cot.at[d, blocks[k], y, :, :, half], cot.at[d, blocks[k], :, x, :, half])[h]
                n = 8 + 2 * k + h
                chunk.hop2[k, h] = go(remote(ref, ref, chunk.send.at[n], chunk.recv.at[n], other))

        def square(chunk, k):
            for h in range(2):
                chunk.hop2[k, h].wait_recv()

        def to_core(chunk, k):
            size = chunk.size // 2
            cols = pl.ds(pl.multiple_of(chunk.at + (1 - d) * size, 256), size)
            ref = cot.at[d, blocks[k], :, :, :, cols]
            chunk.core[k] = go(
                remote(ref, ref, chunk.send.at[16 + k], chunk.recv.at[16 + k], core_peer)
            )

        def sum1(chunk, k):
            for h, near, _, half in both_halves(chunk):
                src = (
                    partial.at[blocks[k], :, 1 - x, :, half],
                    partial.at[blocks[k], 1 - y, :, :, half],
                )[h]
                n = 20 + 2 * k + h
                chunk.sum1[k, h] = go(
                    remote(src, chunk.first.at[h, k], chunk.send.at[n], chunk.recv.at[n], near)
                )

        def sum2(chunk, k):
            for h, _, other, half in both_halves(chunk):
                chunk.sum1[k, h].wait_recv()
                row, column, there = ((1 - y, x, 1 - y), (y, 1 - x, 1 - x))[h]
                total = f32(partial[blocks[k], row, column, :, half]) + f32(chunk.first[h, k, there])
                partial[blocks[k], row, column, :, half] = total.astype(bf16)
                n = 28 + 2 * k + h
                chunk.sum2[k, h] = go(
                    remote(
                        partial.at[blocks[k], row, column, :, half], chunk.second.at[h, k],
                        chunk.send.at[n], chunk.recv.at[n], other,
                    )
                )

        def own_total(chunk, k, h):
            mine = f32(partial[blocks[k], y, x, :, chunk.halves[h]])
            return mine + f32(chunk.first[h, k, (y, x)[h]]) + f32(chunk.second[h, k])

        def square_total(chunk, k):
            for h in range(2):
                chunk.sum2[k, h].wait_recv()
                partial[blocks[k], y, x, :, chunk.halves[h]] = own_total(chunk, k, h).astype(bf16)

        def term(chunk, k):
            if chunk.kind == "z":
                return partial.at[blocks[k], y, x, :, chunk.cols]
            return partial.at[blocks[k], :, :, :, chunk.cols]

        def arrived(chunk, slot):
            ref = chunk.along.at[slot]
            remote(ref, ref, chunk.send.at[41], chunk.recv.at[41 + slot], inner_peer).wait_recv()

        def add_term(chunk, k, slots):
            if chunk.kind == "z":
                total = f32(partial[blocks[k], y, x, :, chunk.cols])
                for slot in slots:
                    total = total + f32(chunk.along[slot])
                partial[blocks[k], y, x, :, chunk.cols] = total.astype(bf16)
                return

            wide = 256

            def step(i, _):
                here = pl.ds(pl.multiple_of(i * wide, wide), wide)
                cols = pl.ds(pl.multiple_of(chunk.at + i * wide, wide), wide)
                total = f32(partial[blocks[k], :, :, :, cols])
                for slot in slots:
                    total = total + f32(chunk.along[slot, :, :, :, here])
                partial[blocks[k], :, :, :, cols] = total.astype(bf16)
                return 0

            lax.fori_loop(0, chunk.size // wide, step, 0)

        def sum_z(chunk, k):
            if is_mid:
                arrived(chunk, k)
                add_term(chunk, k, (k,))

            slot = (None, 4 * mid, end, 2 + end)[k]
            to = along(end * inner + mid * outer) if k == 2 else inner_peer
            ref = term(chunk, k)
            go(remote(ref, chunk.along.at[slot], chunk.send.at[41 + k], chunk.recv.at[41 + slot], to))

        def line_total(chunk):
            arrived(chunk, 0)

            if is_mid:
                arrived(chunk, 4)
                add_term(chunk, 0, (0, 4))

            if not is_mid:
                add_term(chunk, 0, (0,))

        def finish_z(chunk):
            arrived(chunk, 0)
            size = chunk.size // 2

            if is_mid:
                arrived(chunk, 4)

            for h in range(2):
                chunk.sum2[0, h].wait_recv()
                here = pl.ds(h * size, size)
                total = own_total(chunk, 0, h) + f32(chunk.along[0, :, here])

                if is_mid:
                    final[:, chunk.halves[h]] = (total + f32(chunk.along[4, :, here])).astype(bf16)

                if not is_mid:
                    final[:, chunk.halves[h]] = total.astype(bf16)

        def finish_x(chunk):
            for h in range(2):
                chunk.sum2[0, h].wait_recv()
                final[:, chunk.halves[h]] = own_total(chunk, 0, h).astype(bf16)

        graded = [0, 0]

        def hidden_step(step, _):
            cols = pl.ds(pl.multiple_of(step * 128, 128), 128)
            g = f32(gate[:, cols])
            u = f32(up[:, cols])
            value = g * jax.nn.sigmoid(g) * u
            hidden[:, cols] = value.astype(bf16)
            hidden_t[d, cols, :] = value.T.astype(bf16)
            return 0

        def forward(chunk, i):
            base = chunk.at + i * STEP
            cols = pl.ds(base, STEP)
            for b in range(ff // BLOCK):
                keep = jnp.concatenate(
                    [
                        jnp.full((16, BLOCK), f32(mask_ref[b, base // BLOCK + c])).astype(bf16)
                        for c in range(STEP // BLOCK)
                    ],
                    axis=1,
                )
                for r in range(BLOCK // 16):
                    rows = pl.ds(b * BLOCK + r * 16, 16)
                    weight[rows, cols] = weight[rows, cols] * keep
            part = jnp.dot(hidden[...], weight[:, cols], preferred_element_type=jnp.float32)
            partial[:, :, :, :, cols] = part.astype(bf16).reshape(partial.shape[:4] + (STEP,))

        def hidden_grad(chunk, part):
            begin, close = graded[part] == 0, graded[part] == len(CHUNKS) - 1
            graded[part] += 1
            wide = 512

            def step(i, _):
                rows = pl.ds(pl.multiple_of(i * wide, wide), wide)
                back = lax.dot_general(
                    cot[d, :, :, :, :, chunk.cols].reshape(tokens, chunk.size),
                    weight[rows, chunk.cols],
                    (((1,), (1,)), ((), ())),
                    preferred_element_type=jnp.float32,
                )
                if not begin:
                    back = back + acc[:, rows]
                if not close:
                    acc[:, rows] = back
                    return 0
                g = f32(gate[:, rows])
                u = f32(up[:, rows])
                s = jax.nn.sigmoid(g)
                gate_grad[:, rows] = (back * u * s * (1.0 + g * (1.0 - s))).astype(bf16)
                up_grad[:, rows] = (back * (g * s)).astype(bf16)
                return 0

            count = ff // wide // 2
            lax.fori_loop(part * count, (part + 1) * count, step, 0)

        def weight_half(chunk):
            size = chunk.size // 2
            base = pl.multiple_of(chunk.at + d * size, 256)
            cols = pl.ds(base, size)
            total = jnp.zeros((ff, size), jnp.float32)
            for core in range(2):
                total = total + jnp.dot(
                    hidden_t[core],
                    cot[core, :, :, :, :, cols].reshape(tokens, size),
                    preferred_element_type=jnp.float32,
                )
            for b in range(ff // BLOCK):
                for c in range(size // BLOCK):
                    keep = f32(mask_ref[b, chunk.at // BLOCK + d * (size // BLOCK) + c]) * scale
                    block = total[b * BLOCK : (b + 1) * BLOCK, c * BLOCK : (c + 1) * BLOCK]
                    at = pl.ds(pl.multiple_of(base + c * BLOCK, BLOCK), BLOCK)
                    weight_grad[pl.ds(b * BLOCK, BLOCK), at] = (block * keep).astype(bf16)
            chunk.half = go(
                remote(
                    weight_grad.at[:, cols], weight_grad.at[:, cols], chunk.send.at[46],
                    chunk.recv.at[46], core_peer,
                )
            )

        def do_loads():
            loads[0].wait()
            loads[1].wait()

        def do_hidden():
            lax.fori_loop(0, ff // 128, hidden_step, 0)
            hidden_core.start()

        def do_forward(c, i):
            if i == 0:
                weight_loads[c].wait()
            forward(chunks[c], i)

        def do_weight(c, _):
            for k in range(4):
                chunks[c].core[k].wait_recv()
            weight_half(chunks[c])

        actions = {
            "loads": do_loads,
            "hidden": do_hidden,
            "own": lambda: loads[2].wait(),
            "hcore": lambda: hidden_core.wait_recv(),
            "fwd": do_forward,
            "wg": do_weight,
            "hg": lambda c, part: hidden_grad(chunks[c], part),
            "gather": lambda c: gather_z(chunks[c]),
            "pass": lambda c, k: pass_z(chunks[c], k),
            "hop1": lambda c, k: hop1(chunks[c], k),
            "hop2": lambda c, k: hop2(chunks[c], k),
            "square": lambda c, k: square(chunks[c], k),
            "core": lambda c, k: to_core(chunks[c], k),
            "sum1": lambda c, k: sum1(chunks[c], k),
            "sum2": lambda c, k: sum2(chunks[c], k),
            "total": lambda c, k: square_total(chunks[c], k),
            "sumz": lambda c, k: sum_z(chunks[c], k),
            "line": lambda c: line_total(chunks[c]),
            "endz": lambda c: finish_z(chunks[c]),
            "endx": lambda c: finish_x(chunks[c]),
        }
        for name, *args in plan:
            actions[name](*args)

        for chunk in chunks:
            chunk.half.wait_recv()
        for copy in sent:
            copy.wait_send()

        hidden_core.wait_send()

    @pl.when(mid == 1)
    def _():
        run(True, MID_PLAN)

    @pl.when(end == 1)
    def _():
        run(False, END_PLAN)


def keep_in_hbm(array):
    return pltpu.with_memory_space_constraint(array, pltpu.HBM)


def chunk_scratch(rows, width):
    dma = pltpu.SemaphoreType.DMA
    bf16 = jnp.bfloat16
    scratch = []
    for (kind, _), (_, size) in zip(CHUNKS, chunk_columns(width)):
        levels = 4 if kind == "z" else 1
        held = (rows,) if kind == "z" else (2, 2, rows)
        scratch += [
            pltpu.VMEM((2, levels, 2, rows, size // 2), bf16),
            pltpu.VMEM((2, levels, rows, size // 2), bf16),
            pltpu.VMEM((5,) + held + (size,), bf16),
            dma((47,)),
            dma((47,)),
        ]
    return scratch


def fused(gate_pre, up_pre, down_weight, block_mask, out_grad):
    tokens, ff = gate_pre.shape
    rows, width = out_grad.shape
    scale = 1.0 / math.sqrt(tokens * 2)
    hbm = pl.BlockSpec(memory_space=pl.ANY)
    bf16 = jnp.bfloat16
    dma = pltpu.SemaphoreType.DMA
    results = pl.pallas_call(
        functools.partial(fused_kernel, scale),
        out_shape=(
            pltpu.VMEM((rows, width), bf16),
            pltpu.VMEM((tokens, ff), bf16),
            pltpu.VMEM((tokens, ff), bf16),
            pltpu.VMEM((ff, width), bf16),
        ),
        in_specs=[hbm, hbm, hbm, pl.BlockSpec(memory_space=pltpu.SMEM), hbm],
        out_specs=(pl.BlockSpec(memory_space=pltpu.VMEM),) * 4,
        scratch_shapes=[
            pltpu.VMEM((tokens, ff), bf16),
            pltpu.VMEM((tokens, ff), bf16),
            pltpu.VMEM((ff, width), bf16),
            pltpu.VMEM((2, 4, 2, 2, rows, width), bf16),
            pltpu.VMEM((tokens, ff), bf16),
            pltpu.VMEM((2, ff, tokens), bf16),
            pltpu.VMEM((4, 2, 2, rows, width), bf16),
            pltpu.VMEM((tokens, ff), jnp.float32),
            dma((3,)),
            dma((len(CHUNKS),)),
            dma((1,)),
            dma((1,)),
        ]
        + chunk_scratch(rows, width),
        compiler_params=pltpu.CompilerParams(
            collective_id=0, has_side_effects=True, vmem_limit_bytes=50 * 2**20
        ),
        cost_estimate=pl.CostEstimate(
            flops=8 * tokens * ff * width, bytes_accessed=40 * 2**20, transcendentals=2 * tokens * ff
        ),
    )(*(keep_in_hbm(a) for a in (gate_pre, up_pre, down_weight)), block_mask, keep_in_hbm(out_grad))
    return hand_on(results)


def hand_on_kernel(arrays, *refs):
    srcs, dsts, store_sem = refs[:arrays], refs[arrays : 2 * arrays], refs[2 * arrays]
    stores = [
        pltpu.make_async_copy(src, dst, store_sem.at[n])
        for n, (src, dst) in enumerate(zip(srcs, dsts))
    ]
    for store in stores:
        store.start()
    for store in stores:
        store.wait()


def hand_on(arrays):
    return pl.pallas_call(
        functools.partial(hand_on_kernel, len(arrays)),
        out_shape=tuple(jax.ShapeDtypeStruct(a.shape, a.dtype) for a in arrays),
        in_specs=[pl.BlockSpec(memory_space=pltpu.VMEM)] * len(arrays),
        out_specs=(pl.BlockSpec(memory_space=pl.ANY),) * len(arrays),
        scratch_shapes=[pltpu.SemaphoreType.DMA((len(arrays),))],
        compiler_params=pltpu.CompilerParams(vmem_limit_bytes=2 * 2**20),
    )(*(pltpu.with_memory_space_constraint(a, pltpu.VMEM) for a in arrays))


def local(gate_pre, up_pre, down_weight, block_mask, out_grad):
    blk_rows, blk_cols = block_mask.shape
    ff_local, width = down_weight.shape
    masked = (
        down_weight.reshape(blk_rows, 128, blk_cols, 128)
        * block_mask.astype(jnp.bfloat16)[:, None, :, None]
    ).reshape(ff_local, width)
    gate_val = gate_pre.astype(jnp.float32)
    up_val = up_pre.astype(jnp.float32)
    sigmoid_gate = jax.nn.sigmoid(gate_val)
    silu_gate = gate_val * sigmoid_gate
    hidden = (silu_gate * up_val).astype(jnp.bfloat16)
    layer_out = lax.psum_scatter(
        jnp.dot(hidden, masked, preferred_element_type=jnp.float32),
        "tensor",
        scatter_dimension=0,
        tiled=True,
    ).astype(jnp.bfloat16)
    cot_rows = lax.all_gather(out_grad, "tensor", axis=0, tiled=True)
    hidden_grad = lax.dot_general(
        cot_rows, masked, (((1,), (1,)), ((), ())), preferred_element_type=jnp.float32
    )
    gate_grad = (
        hidden_grad * up_val * sigmoid_gate * (1.0 + gate_val * (1.0 - sigmoid_gate))
    ).astype(jnp.bfloat16)
    up_grad = (hidden_grad * silu_gate).astype(jnp.bfloat16)
    tokens_all = out_grad.shape[0] * lax.axis_size("tensor") * lax.axis_size("dp")
    grad_scale = 1.0 / math.sqrt(tokens_all)
    partial_grad = (
        lax.dot_general(
            hidden, cot_rows, (((0,), (0,)), ((), ())), preferred_element_type=jnp.float32
        )
        * grad_scale
    )
    blocked = (
        partial_grad.reshape(blk_rows, 128, blk_cols, 128)
        * block_mask.astype(jnp.float32)[:, None, :, None]
    )
    summed = lax.psum(blocked.reshape(ff_local, width), "dp")
    weight_grad = summed.astype(jnp.bfloat16)
    return (layer_out, gate_grad, up_grad, weight_grad)


def solution(mesh):
    grouped = mesh.shape["dp"] == 2 and mesh.shape["tensor"] == 16
    return jax.shard_map(
        fused if grouped else local,
        mesh=mesh,
        in_specs=(
            P("dp", "tensor"),
            P("dp", "tensor"),
            P("tensor", None),
            P("tensor", None),
            P(("dp", "tensor"), None),
        ),
        out_specs=(
            P(("dp", "tensor"), None),
            P("dp", "tensor"),
            P("dp", "tensor"),
            P("tensor", None),
        ),
        check_vma=False,
    )
```

time: 82.6 us -> 70.1 us (0.85)
  Pallas kernels: 81.6 us -> 69 us
    pallas_call x1, Pallas kernels: 77.4 us -> 64.8 us  [fused(): pl.pallas_call(functools.partial(fused_kernel, scale), out_shape=(pltpu.V...]
where the time goes in v4:
time: 70.1 us; the launch traced here: 69.9 us
  Pallas kernels  69 us (98%)
  between operations  0.86 us (1%)
    pallas_call x1, Pallas kernels, fused(): pl.pallas_call(functools.partial(fused_kernel, scale), out_shape=(pltpu.V...  64.8 us
    pallas_call x1, Pallas kernels, hand_on(): pl.pallas_call(functools.partial(hand_on_kernel, len(arrays)), out_shape=...  4.21 us

profile of v4, /device:TPU:0, one launch (start us, length us, event | category | flops | bytes accessed | tf_op | source)
XLA Modules:
  0.0 69.9 jit_solution(3703065926044995263)
XLA Ops:
  0.6 64.8 %shard_map.84 = (bf16[32,4096]{1,0:T(8,128)(2,1)S(1)}, bf16[512,1024]{1,0:T(8,128)(2,1)S(1)}, bf16[512,1024]{1,0:T(8,128)(2,1)S(1)}, bf16[1024,4096]{1,0:T(8,128)(2,1)S(1)}) custom-call(bf16[512,1024]{1,0:T(8,128)(2,1)} %gate_hbm.1, bf16[512,1024]{1,0:T(8,128)(2,1)} %up_hbm.1, bf16[1024,4096]{1,0:T(8,128)(2,1)} %weight_hbm.1, s32[8,32]{1,0:T(8,128)} %mask_ref.1, ...), custom_call_target="tpu_custom_call" | custom-call | flops 17179869184 | bytes 41943040 | tf_op jit(solution)/shard_map/pallas_call | solution.py:537
  65.4 4.2 %shard_map.85 = (bf16[32,4096]{1,0:T(8,128)(2,1)}, bf16[512,1024]{1,0:T(8,128)(2,1)}, bf16[512,1024]{1,0:T(8,128)(2,1)}, bf16[1024,4096]{1,0:T(8,128)(2,1)}) custom-call(bf16[32,4096]{1,0:T(8,128)(2,1)S(1)} %get-tuple-element.8.refs_0_, bf16[512,1024]{1,0:T(8,128)(2,1)S(1)} %get-tuple-element.9.refs_1_, bf16[512,1024]{1,0:T(8,128)(2,1)S(1)} %get-tuple-element.10.refs_2_, ...), custom_call_target="tpu_custom_call" | custom-call | tf_op jit(solution)/shard_map/pallas_call | solution.py:585

commit v5 on v4

--- a/solution.py
+++ b/solution.py
@@ -10,83 +10,77 @@
 
 BLOCK = 128
 STEP = 512
-CHUNKS = (("z", 1), ("z", 2), ("z", 2), ("x", 1), ("x", 1), ("x", 1))
+CHUNKS = (("z", 2), ("z", 2), ("z", 1), ("x", 1), ("x", 2))
 CHUNK_SCRATCH = 5
 
 
-FORWARD = (1, 4, 0, 5, 2, 3)
+FORWARD = (2, 0, 1, 4, 3)
+LATE = (3, )
 MID_PLAN = (
-    ("hop1", 3, 0), ("hop1", 4, 0), ("gather", 0), ("gather", 2), ("hop1", 5, 0), ("hop1", 1, 0),
-    ("gather", 1), ("hop1", 0, 0), ("hop1", 2, 0), ("own",), ("hop2", 3, 0), ("pass", 0, 0),
-    ("pass", 0, 1), ("hop1", 0, 1), ("hop2", 5, 0), ("hop2", 1, 0), ("pass", 2, 0),
-    ("pass", 1, 1), ("hop1", 0, 2), ("pass", 1, 0), ("hop1", 1, 1), ("hop2", 4, 0),
-    ("square", 3, 0), ("hop1", 2, 1), ("pass", 0, 2), ("pass", 2, 1), ("hop1", 2, 2), ("loads",),
-    ("gather", 3), ("hidden",), ("square", 5, 0), ("pass", 1, 2), ("square", 1, 0),
-    ("hop2", 0, 1), ("hop2", 2, 0), ("fwd", 1, 0), ("gather", 5), ("hop1", 0, 3), ("hop2", 0, 0),
-    ("pass", 2, 2), ("core", 5, 0), ("fwd", 4, 0), ("fwd", 0, 0), ("hop1", 1, 2), ("fwd", 5, 0),
-    ("square", 4, 0), ("pass", 3, 1), ("hop2", 2, 2), ("hcore",), ("hop1", 2, 3), ("core", 4, 0),
-    ("pass", 3, 0), ("fwd", 2, 0), ("fwd", 2, 1), ("hop2", 1, 1), ("hop1", 1, 3),
-    ("square", 0, 0), ("pass", 5, 0), ("pass", 5, 1), ("fwd", 1, 1), ("hop2", 2, 1),
-    ("pass", 4, 1), ("hop2", 0, 3), ("pass", 3, 2), ("sumz", 4, 3), ("hop2", 2, 3), ("gather", 4),
-    ("square", 1, 1), ("core", 3, 3), ("hop2", 1, 3), ("sum1", 0, 3), ("sum1", 2, 1),
-    ("pass", 5, 2), ("square", 2, 0), ("hop2", 1, 2), ("square", 2, 3), ("hg", 5, 0),
-    ("sum1", 2, 3), ("sum2", 0, 3), ("hop2", 0, 2), ("fwd", 3, 0), ("sum1", 0, 2), ("sum1", 1, 1),
-    ("sumz", 3, 3), ("square", 2, 2), ("sum1", 1, 2), ("hg", 5, 1), ("sum2", 2, 1),
-    ("sumz", 5, 3), ("square", 1, 3), ("core", 0, 0), ("core", 1, 0), ("square", 2, 1),
-    ("square", 0, 3), ("square", 0, 1), ("hg", 2, 0), ("pass", 4, 0), ("core", 1, 3),
-    ("square", 1, 2), ("sum1", 0, 1), ("total", 0, 3), ("sum1", 1, 3), ("sum1", 2, 0),
-    ("core", 5, 1), ("sumz", 4, 1), ("core", 5, 3), ("hg", 1, 0), ("core", 2, 3), ("hg", 3, 0),
-    ("sumz", 4, 2), ("core", 4, 1), ("sumz", 3, 1), ("square", 0, 2), ("sumz", 3, 2),
-    ("hg", 2, 1), ("core", 2, 0), ("core", 2, 2), ("hg", 3, 1), ("hg", 0, 0), ("core", 2, 1),
-    ("core", 0, 2), ("core", 1, 1), ("core", 1, 2), ("core", 3, 1), ("sum2", 0, 2),
-    ("sumz", 5, 2), ("sum2", 2, 3), ("pass", 4, 2), ("core", 3, 0), ("hg", 4, 0), ("core", 3, 2),
-    ("sumz", 5, 1), ("sum2", 1, 2), ("sum2", 1, 3), ("core", 4, 3), ("core", 4, 2),
-    ("core", 0, 3), ("sum2", 0, 1), ("sumz", 0, 3), ("sum1", 2, 2), ("total", 2, 1), ("line", 4),
-    ("sum1", 4, 0), ("sum1", 1, 0), ("hg", 0, 1), ("hg", 1, 1), ("sum2", 1, 1), ("wg", 2, 0),
-    ("total", 1, 3), ("sumz", 1, 3), ("wg", 4, 0), ("total", 1, 2), ("total", 0, 2), ("line", 3),
-    ("total", 2, 3), ("sum1", 3, 0), ("total", 0, 1), ("sum2", 2, 2), ("core", 0, 1),
-    ("sumz", 2, 3), ("core", 5, 2), ("wg", 1, 0), ("sum1", 0, 0), ("line", 5), ("sum1", 5, 0),
-    ("sum2", 2, 0), ("sum2", 1, 0), ("sumz", 0, 1), ("sumz", 2, 1), ("sumz", 0, 2),
-    ("sum2", 4, 0), ("sumz", 1, 2), ("sum2", 3, 0), ("total", 1, 1), ("wg", 0, 0),
-    ("total", 2, 2), ("sumz", 2, 2), ("sumz", 1, 1), ("wg", 3, 0), ("sum2", 0, 0), ("sum2", 5, 0),
-    ("wg", 5, 0), ("hg", 4, 1), ("endz", 0), ("endz", 1), ("endz", 2), ("endx", 4), ("endx", 3),
-    ("endx", 5),
+    ("gather", 1), ("hop1", 4, 0), ("gather", 2), ("hop1", 3, 0), ("hop1", 1, 0), ("own",),
+    ("hop1", 0, 0), ("hop1", 2, 0), ("gather", 0), ("hop2", 4, 0), ("pass", 1, 0), ("pass", 2, 1),
+    ("pass", 1, 1), ("pass", 2, 0), ("loads",), ("hop2", 3, 0), ("hop1", 1, 1), ("pass", 0, 0),
+    ("pass", 0, 1), ("hop1", 1, 2), ("hop2", 0, 0), ("pass", 2, 2), ("hop1", 0, 1),
+    ("hop1", 2, 1), ("square", 4, 0), ("gather", 4), ("hop1", 2, 2), ("hidden",), ("hop2", 1, 1),
+    ("square", 3, 0), ("pass", 1, 2), ("hop1", 1, 3), ("fwd", 2, 0), ("fwd", 0, 0),
+    ("hop1", 2, 3), ("hop1", 0, 2), ("gather", 3), ("hop2", 0, 1), ("pass", 0, 2), ("hop2", 2, 1),
+    ("fwd", 0, 1), ("sum1", 2, 3), ("fwd", 1, 0), ("sum1", 2, 1), ("fwd", 4, 0), ("pass", 4, 0),
+    ("sum1", 0, 3), ("square", 1, 1), ("pass", 4, 1), ("fwd", 4, 1), ("hop2", 1, 2),
+    ("core", 1, 1), ("hop1", 0, 3), ("sum2", 2, 1), ("hop2", 0, 2), ("fwd", 1, 1), ("pass", 3, 1),
+    ("fwd", 3, 0), ("sumz", 3, 3), ("hop2", 1, 0), ("core", 4, 1), ("sum1", 2, 2), ("hop2", 1, 3),
+    ("core", 3, 2), ("sum1", 1, 2), ("pass", 4, 2), ("hop2", 0, 3), ("sumz", 3, 1),
+    ("pass", 3, 2), ("square", 0, 2), ("core", 4, 3), ("core", 4, 0), ("pass", 3, 0),
+    ("core", 4, 2), ("sum1", 1, 1), ("square", 0, 0), ("hcore",), ("square", 1, 2),
+    ("sum2", 2, 2), ("core", 0, 2), ("square", 1, 0), ("core", 0, 0), ("square", 1, 3),
+    ("sum1", 0, 1), ("sum1", 1, 0), ("sum2", 2, 3), ("hg", 3, 0), ("sumz", 4, 3), ("hg", 4, 0),
+    ("wg", 4, 0), ("hop2", 2, 0), ("square", 0, 3), ("core", 1, 0), ("core", 1, 2),
+    ("core", 1, 3), ("hg", 3, 1), ("sum1", 1, 3), ("sumz", 3, 2), ("sum2", 1, 1),
+    ("square", 0, 1), ("sum1", 0, 2), ("total", 2, 1), ("sum2", 0, 1), ("hg", 1, 0),
+    ("sumz", 4, 1), ("hg", 4, 1), ("hop2", 2, 3), ("core", 0, 1), ("square", 2, 0),
+    ("sum2", 0, 3), ("line", 3), ("total", 2, 3), ("sumz", 2, 3), ("sumz", 4, 2), ("core", 0, 3),
+    ("hg", 0, 0), ("sum2", 1, 2), ("sum2", 1, 3), ("wg", 1, 0), ("square", 2, 1), ("hop2", 2, 2),
+    ("sum1", 2, 0), ("core", 3, 1), ("sum2", 0, 2), ("wg", 0, 0), ("sum1", 3, 0), ("line", 4),
+    ("total", 2, 2), ("total", 1, 3), ("core", 3, 3), ("sumz", 1, 3), ("total", 0, 3),
+    ("sum1", 0, 0), ("square", 2, 3), ("core", 3, 0), ("core", 2, 3), ("sumz", 2, 2),
+    ("sumz", 0, 3), ("core", 2, 1), ("sum1", 4, 0), ("square", 2, 2), ("core", 2, 2),
+    ("core", 2, 0), ("total", 0, 1), ("total", 1, 1), ("hg", 2, 0), ("sum2", 2, 0),
+    ("sumz", 1, 1), ("hg", 1, 1), ("sum2", 1, 0), ("total", 0, 2), ("total", 1, 2),
+    ("sumz", 1, 2), ("wg", 3, 0), ("sum2", 3, 0), ("sum2", 0, 0), ("sumz", 0, 1), ("wg", 2, 0),
+    ("sumz", 0, 2), ("sum2", 4, 0), ("sumz", 2, 1), ("hg", 2, 1), ("hg", 0, 1), ("endx", 3),
+    ("endz", 0), ("endx", 4), ("endz", 1), ("endz", 2),
 )
 END_PLAN = (
-    ("hop1", 3, 0), ("gather", 0), ("hop1", 5, 0), ("hop1", 1, 0), ("own",), ("hop1", 0, 0),
-    ("gather", 1), ("hop1", 4, 0), ("gather", 2), ("hop1", 2, 0), ("loads",), ("hidden",),
-    ("hop2", 5, 0), ("hop2", 3, 0), ("fwd", 4, 0), ("hop2", 1, 0), ("sumz", 4, 3), ("hop2", 4, 0),
-    ("pass", 0, 0), ("fwd", 2, 0), ("fwd", 2, 1), ("pass", 2, 0), ("sum1", 2, 3), ("fwd", 0, 0),
-    ("square", 5, 0), ("pass", 1, 0), ("sum1", 0, 2), ("square", 3, 0), ("hop1", 1, 1),
-    ("pass", 0, 1), ("gather", 3), ("gather", 5), ("hop1", 0, 1), ("pass", 2, 1), ("fwd", 3, 0),
-    ("core", 3, 0), ("hop1", 0, 2), ("hcore",), ("square", 4, 0), ("hop2", 2, 0), ("fwd", 5, 0),
-    ("hop1", 2, 2), ("gather", 4), ("pass", 1, 1), ("sum2", 0, 2), ("hop2", 1, 1), ("hop1", 1, 2),
-    ("pass", 3, 0), ("pass", 0, 2), ("hop2", 0, 0), ("hop2", 0, 1), ("sum1", 0, 3),
-    ("pass", 1, 2), ("hop1", 1, 3), ("sumz", 5, 3), ("sumz", 4, 2), ("sum1", 2, 2),
-    ("square", 0, 1), ("hop2", 1, 2), ("sum2", 2, 3), ("square", 1, 0), ("hop2", 1, 3),
-    ("sumz", 3, 3), ("square", 2, 0), ("sumz", 3, 2), ("pass", 2, 2), ("fwd", 1, 0),
-    ("pass", 3, 1), ("core", 1, 0), ("hop1", 0, 3), ("sumz", 4, 1), ("fwd", 1, 1), ("pass", 5, 0),
-    ("sum1", 1, 3), ("sum1", 0, 1), ("square", 1, 1), ("hop1", 2, 1), ("square", 1, 2),
-    ("pass", 5, 1), ("sumz", 5, 2), ("total", 0, 2), ("core", 3, 2), ("hop2", 0, 3),
-    ("hop2", 0, 2), ("sum2", 1, 3), ("square", 1, 3), ("core", 1, 2), ("sum1", 1, 2),
-    ("sumz", 3, 1), ("sum2", 0, 3), ("hg", 1, 0), ("core", 5, 1), ("core", 1, 1), ("hop1", 2, 3),
-    ("total", 2, 3), ("hop2", 2, 1), ("square", 0, 2), ("sum2", 2, 2), ("pass", 3, 2),
-    ("core", 5, 2), ("total", 1, 3), ("hg", 3, 0), ("hg", 3, 1), ("core", 1, 3), ("sum2", 1, 2),
-    ("pass", 5, 2), ("pass", 4, 0), ("hop2", 2, 2), ("hg", 5, 0), ("core", 5, 0), ("hg", 5, 1),
-    ("square", 0, 0), ("sum1", 1, 1), ("sum2", 0, 1), ("total", 0, 3), ("hop2", 2, 3),
-    ("core", 3, 1), ("core", 2, 0), ("sumz", 0, 3), ("square", 0, 3), ("core", 0, 3),
-    ("core", 5, 3), ("core", 0, 1), ("sumz", 1, 3), ("sumz", 2, 3), ("core", 0, 2),
-    ("core", 3, 3), ("sumz", 5, 1), ("wg", 1, 0), ("sum1", 2, 1), ("total", 2, 2), ("sumz", 2, 2),
-    ("hg", 0, 0), ("core", 4, 1), ("sum1", 2, 0), ("square", 2, 1), ("hg", 0, 1), ("core", 0, 0),
-    ("wg", 3, 0), ("wg", 5, 0), ("wg", 0, 0), ("core", 2, 1), ("sum1", 1, 0), ("square", 2, 2),
-    ("total", 1, 2), ("total", 0, 1), ("sumz", 0, 2), ("line", 3), ("sum2", 1, 1), ("sum1", 0, 0),
-    ("sum1", 3, 0), ("pass", 4, 1), ("square", 2, 3), ("core", 2, 2), ("core", 2, 3),
-    ("sumz", 0, 1), ("line", 4), ("hg", 1, 1), ("sum2", 2, 1), ("sumz", 1, 2), ("line", 5),
-    ("sum1", 5, 0), ("core", 4, 2), ("sum1", 4, 0), ("wg", 2, 0), ("hg", 2, 0), ("pass", 4, 2),
-    ("sum2", 2, 0), ("core", 4, 0), ("total", 1, 1), ("sumz", 1, 1), ("core", 4, 3),
-    ("sum2", 1, 0), ("hg", 4, 0), ("sum2", 3, 0), ("total", 2, 1), ("sum2", 0, 0), ("sumz", 2, 1),
-    ("wg", 4, 0), ("sum2", 5, 0), ("sum2", 4, 0), ("hg", 4, 1), ("hg", 2, 1), ("endz", 1),
-    ("endz", 2), ("endx", 3), ("endx", 5), ("endz", 0), ("endx", 4),
+    ("hop1", 3, 0), ("gather", 2), ("hop1", 4, 0), ("hop1", 1, 0), ("hop1", 2, 0), ("gather", 1),
+    ("own",), ("gather", 0), ("hop1", 0, 0), ("loads",), ("hidden",), ("hop2", 4, 0),
+    ("fwd", 3, 0), ("sumz", 3, 1), ("hop2", 3, 0), ("fwd", 2, 0), ("sum1", 2, 1), ("pass", 1, 0),
+    ("pass", 2, 0), ("hop2", 1, 0), ("fwd", 4, 0), ("pass", 0, 0), ("fwd", 1, 0),
+    ("square", 4, 0), ("gather", 4), ("hop1", 2, 1), ("sum1", 2, 3), ("square", 3, 0),
+    ("gather", 3), ("hop1", 0, 1), ("hop1", 1, 1), ("pass", 2, 1), ("fwd", 0, 0), ("sum1", 2, 2),
+    ("hop2", 2, 0), ("pass", 2, 2), ("hop1", 2, 3), ("hop2", 0, 0), ("pass", 0, 1),
+    ("square", 1, 0), ("sumz", 3, 3), ("fwd", 1, 1), ("sum2", 2, 2), ("sum2", 2, 1),
+    ("sum2", 2, 3), ("sum1", 1, 3), ("sumz", 3, 2), ("hop2", 2, 3), ("fwd", 4, 1), ("hop1", 2, 2),
+    ("fwd", 0, 1), ("hop1", 0, 2), ("square", 0, 0), ("sumz", 4, 3), ("sum1", 0, 3),
+    ("pass", 4, 0), ("sum1", 1, 2), ("sum1", 0, 2), ("hop2", 2, 1), ("hop2", 0, 1),
+    ("pass", 0, 2), ("hop2", 0, 2), ("hop1", 0, 3), ("sumz", 4, 2), ("sum1", 0, 1),
+    ("pass", 4, 1), ("sum2", 0, 3), ("square", 0, 2), ("square", 2, 3), ("sum2", 1, 2),
+    ("hop2", 2, 2), ("total", 2, 3), ("core", 3, 0), ("pass", 1, 1), ("core", 4, 0),
+    ("core", 2, 3), ("sumz", 2, 3), ("sum2", 1, 3), ("square", 0, 1), ("hop2", 0, 3),
+    ("pass", 1, 2), ("square", 2, 1), ("hop2", 1, 1), ("core", 4, 1), ("total", 1, 2), ("hcore",),
+    ("pass", 4, 2), ("hop1", 1, 2), ("core", 2, 1), ("sumz", 4, 1), ("hop1", 1, 3),
+    ("sum2", 0, 2), ("hg", 4, 0), ("total", 1, 3), ("hg", 4, 1), ("pass", 3, 0), ("square", 2, 0),
+    ("core", 4, 3), ("core", 4, 2), ("core", 0, 0), ("square", 2, 2), ("sum1", 1, 1),
+    ("total", 2, 1), ("sum1", 2, 0), ("sumz", 1, 3), ("core", 2, 2), ("total", 0, 3),
+    ("square", 0, 3), ("total", 2, 2), ("hg", 0, 0), ("hg", 0, 1), ("sum2", 0, 1), ("core", 2, 0),
+    ("core", 0, 2), ("hop2", 1, 3), ("sumz", 0, 3), ("hop2", 1, 2), ("core", 0, 1),
+    ("core", 0, 3), ("wg", 4, 0), ("hg", 2, 0), ("sumz", 1, 2), ("pass", 3, 1), ("sum2", 1, 1),
+    ("square", 1, 1), ("wg", 0, 0), ("sum1", 0, 0), ("total", 0, 2), ("line", 3), ("sumz", 2, 1),
+    ("sumz", 0, 2), ("total", 0, 1), ("sum1", 3, 0), ("core", 3, 1), ("sum1", 1, 0),
+    ("sum2", 2, 0), ("pass", 3, 2), ("core", 3, 3), ("wg", 2, 0), ("core", 1, 0), ("hg", 3, 0),
+    ("hg", 2, 1), ("square", 1, 2), ("sumz", 2, 2), ("total", 1, 1), ("square", 1, 3),
+    ("core", 3, 2), ("core", 1, 2), ("sumz", 0, 1), ("core", 1, 1), ("sumz", 1, 1),
+    ("core", 1, 3), ("line", 4), ("sum1", 4, 0), ("hg", 1, 0), ("sum2", 0, 0), ("wg", 3, 0),
+    ("sum2", 3, 0), ("sum2", 1, 0), ("wg", 1, 0), ("sum2", 4, 0), ("endz", 2), ("hg", 1, 1),
+    ("hg", 3, 1), ("endz", 0), ("endx", 3), ("endz", 1), ("endx", 4),
 )
 
 
@@ -117,8 +111,8 @@
 def fused_kernel(
     scale,
     gate_hbm, up_hbm, weight_hbm, mask_ref, grad_hbm,
-    final, gate_grad, up_grad, weight_grad,
-    gate, up, weight, cot, hidden, hidden_t, partial, acc,
+    final, gate_grad, up_grad, weight_grad, cot, hidden_t,
+    gate, up, weight, hidden, partial, acc,
     in_sem, weight_sem, hidden_send, hidden_recv,
     *scratch,
 ):
@@ -202,6 +196,7 @@
             at, size = spans[c]
             chunk.kind, chunk.at, chunk.size = kind, at, size
             chunk.cols = pl.ds(at, size)
+            chunk.late = c in LATE
             chunk.halves = (pl.ds(at, size // 2), pl.ds(at + size // 2, size // 2))
             chunk.first, chunk.second, chunk.along, chunk.send, chunk.recv = scratch[
                 CHUNK_SCRATCH * c : CHUNK_SCRATCH * (c + 1)
@@ -255,6 +250,8 @@
         def to_core(chunk, k):
             size = chunk.size // 2
             cols = pl.ds(pl.multiple_of(chunk.at + (1 - d) * size, 256), size)
+            if chunk.late:
+                cols = chunk.cols
             ref = cot.at[d, blocks[k], :, :, :, cols]
             chunk.core[k] = go(
                 remote(ref, ref, chunk.send.at[16 + k], chunk.recv.at[16 + k], core_peer)
@@ -463,7 +460,8 @@
         def do_weight(c, _):
             for k in range(4):
                 chunks[c].core[k].wait_recv()
-            weight_half(chunks[c])
+            if not chunks[c].late:
+                weight_half(chunks[c])
 
         actions = {
             "loads": do_loads,
@@ -491,7 +489,8 @@
             actions[name](*args)
 
         for chunk in chunks:
-            chunk.half.wait_recv()
+            if not chunk.late:
+                chunk.half.wait_recv()
         for copy in sent:
             copy.wait_send()
 
@@ -541,16 +540,16 @@
             pltpu.VMEM((tokens, ff), bf16),
             pltpu.VMEM((tokens, ff), bf16),
             pltpu.VMEM((ff, width), bf16),
+            pltpu.VMEM((2, 4, 2, 2, rows, width), bf16),
+            pltpu.VMEM((2, ff, tokens), bf16),
         ),
         in_specs=[hbm, hbm, hbm, pl.BlockSpec(memory_space=pltpu.SMEM), hbm],
-        out_specs=(pl.BlockSpec(memory_space=pltpu.VMEM),) * 4,
+        out_specs=(pl.BlockSpec(memory_space=pltpu.VMEM),) * 6,
         scratch_shapes=[
             pltpu.VMEM((tokens, ff), bf16),
             pltpu.VMEM((tokens, ff), bf16),
             pltpu.VMEM((ff, width), bf16),
-            pltpu.VMEM((2, 4, 2, 2, rows, width), bf16),
             pltpu.VMEM((tokens, ff), bf16),
-            pltpu.VMEM((2, ff, tokens), bf16),
             pltpu.VMEM((4, 2, 2, rows, width), bf16),
             pltpu.VMEM((tokens, ff), jnp.float32),
             dma((3,)),
@@ -560,36 +559,88 @@
         ]
         + chunk_scratch(rows, width),
         compiler_params=pltpu.CompilerParams(
-            collective_id=0, has_side_effects=True, vmem_limit_bytes=50 * 2**20
+            collective_id=0, has_side_effects=True, vmem_limit_bytes=38 * 2**20
         ),
         cost_estimate=pl.CostEstimate(
             flops=8 * tokens * ff * width, bytes_accessed=40 * 2**20, transcendentals=2 * tokens * ff
         ),
-    )(*(keep_in_hbm(a) for a in (gate_pre, up_pre, down_weight)), block_mask, keep_in_hbm(out_grad))
-    return hand_on(results)
-
-
-def hand_on_kernel(arrays, *refs):
-    srcs, dsts, store_sem = refs[:arrays], refs[arrays : 2 * arrays], refs[2 * arrays]
-    stores = [
-        pltpu.make_async_copy(src, dst, store_sem.at[n])
-        for n, (src, dst) in enumerate(zip(srcs, dsts))
-    ]
-    for store in stores:
-        store.start()
-    for store in stores:
-        store.wait()
-
-
-def hand_on(arrays):
+    )(*(keep_in_hbm(a) for a in (gate_pre, up_pre, down_weight, block_mask, out_grad)))
+    return hand_on(scale, block_mask, *results)
+
+
+def hand_on_kernel(
+    scale, mask_hbm, final, gate_grad, up_grad, weight_grad, cot, hidden_t,
+    final_hbm, gate_grad_hbm, up_grad_hbm, weight_grad_hbm, mask_ref, tile, store_sem, mask_sem,
+):
+    ff, width = weight_grad.shape
+    tokens = hidden_t.shape[2]
+    spans = chunk_columns(width)
+    stores = []
+
+    def store(src, dst):
+        copy = pltpu.make_async_copy(src, dst, store_sem.at[len(stores)])
+        copy.start()
+        stores.append(copy)
+
+    mask_load = pltpu.make_async_copy(mask_hbm, mask_ref, mask_sem.at[0])
+    mask_load.start()
+    runs = []
+    for c, (at, size) in enumerate(spans):
+        if c in LATE:
+            continue
+        if runs and sum(runs[-1]) == at:
+            at, size = runs[-1][0], runs[-1][1] + size
+            runs.pop()
+        runs.append((at, size))
+    for at, size in runs:
+        store(weight_grad.at[:, pl.ds(at, size)], weight_grad_hbm.at[:, pl.ds(at, size)])
+    store(gate_grad, gate_grad_hbm)
+    store(up_grad, up_grad_hbm)
+    store(final, final_hbm)
+    wide = 512
+    put = 0
+    mask_load.wait()
+    for c in LATE:
+        at, size = spans[c]
+        for first in range(at, at + size, wide):
+            cols = pl.ds(first, wide)
+            total = jnp.zeros((ff, wide), jnp.float32)
+            for core in range(2):
+                total = total + jnp.dot(
+                    hidden_t[core],
+                    cot[core, :, :, :, :, cols].reshape(tokens, wide),
+                    preferred_element_type=jnp.float32,
+                )
+            for b in range(ff // BLOCK):
+                for n in range(wide // BLOCK):
+                    keep = f32(mask_ref[b, first // BLOCK + n]) * scale
+                    block = total[b * BLOCK : (b + 1) * BLOCK, n * BLOCK : (n + 1) * BLOCK]
+                    tile[pl.ds(b * BLOCK, BLOCK), pl.ds(put + n * BLOCK, BLOCK)] = (
+                        block * keep
+                    ).astype(jnp.bfloat16)
+            store(tile.at[:, pl.ds(put, wide)], weight_grad_hbm.at[:, cols])
+            put += wide
+    for copy in stores:
+        copy.wait()
+
+
+def hand_on(scale, block_mask, *arrays):
+    ff, width = arrays[3].shape
+    late = sum(chunk_columns(width)[c][1] for c in LATE)
+    held = pl.BlockSpec(memory_space=pltpu.VMEM)
     return pl.pallas_call(
-        functools.partial(hand_on_kernel, len(arrays)),
-        out_shape=tuple(jax.ShapeDtypeStruct(a.shape, a.dtype) for a in arrays),
-        in_specs=[pl.BlockSpec(memory_space=pltpu.VMEM)] * len(arrays),
-        out_specs=(pl.BlockSpec(memory_space=pl.ANY),) * len(arrays),
-        scratch_shapes=[pltpu.SemaphoreType.DMA((len(arrays),))],
-        compiler_params=pltpu.CompilerParams(vmem_limit_bytes=2 * 2**20),
-    )(*(pltpu.with_memory_space_constraint(a, pltpu.VMEM) for a in arrays))
+        functools.partial(hand_on_kernel, scale),
+        out_shape=tuple(jax.ShapeDtypeStruct(a.shape, a.dtype) for a in arrays[:4]),
+        in_specs=[pl.BlockSpec(memory_space=pl.ANY)] + [held] * len(arrays),
+        out_specs=(pl.BlockSpec(memory_space=pl.ANY),) * 4,
+        scratch_shapes=[
+            pltpu.SMEM(block_mask.shape, jnp.int32),
+            pltpu.VMEM((ff, late), jnp.bfloat16),
+            pltpu.SemaphoreType.DMA((len(CHUNKS) + 3 + late // 512,)),
+            pltpu.SemaphoreType.DMA((1,)),
+        ],
+        compiler_params=pltpu.CompilerParams(vmem_limit_bytes=12 * 2**20),
+    )(keep_in_hbm(block_mask), *(pltpu.with_memory_space_constraint(a, pltpu.VMEM) for a in arrays))
 
 
 def local(gate_pre, up_pre, down_weight, block_mask, out_grad):

time: 70.1 us -> 69 us (0.984)
  Pallas kernels: 69 us -> 67.9 us
    pallas_call x1, Pallas kernels: 64.8 us -> 63.8 us  [fused(): pl.pallas_call(functools.partial(fused_kernel, scale), out_shape=(pltpu.V...]
where the time goes in v5:
time: 69 us; the launch traced here: 68.8 us
  Pallas kernels  67.9 us (98%)
  between operations  0.86 us (1%)
    pallas_call x1, Pallas kernels, fused(): pl.pallas_call(functools.partial(fused_kernel, scale), out_shape=(pltpu.V...  63.8 us
    pallas_call x1, Pallas kernels, hand_on(): pl.pallas_call(functools.partial(hand_on_kernel, scale), out_shape=tuple(...  4.13 us

profile of v5, /device:TPU:0, one launch (start us, length us, event | category | flops | bytes accessed | tf_op | source)
XLA Modules:
  0.0 68.8 jit_solution(11106813462731310985)
XLA Ops:
  0.6 63.8 %shard_map.84 = (bf16[32,4096]{1,0:T(8,128)(2,1)S(1)}, bf16[512,1024]{1,0:T(8,128)(2,1)S(1)}, bf16[512,1024]{1,0:T(8,128)(2,1)S(1)}, bf16[1024,4096]{1,0:T(8,128...) custom-call(bf16[512,1024]{1,0:T(8,128)(2,1)} %gate_hbm.1, ...), custom_call_target="tpu_custom_call" | custom-call | flops 17179869184 | bytes 41943040 | tf_op jit(solution)/shard_map/pallas_call | solution.py:536
  64.4 4.1 %shard_map.85 = (bf16[32,4096]{1,0:T(8,128)(2,1)}, bf16[512,1024]{1,0:T(8,128)(2,1)}, bf16[512,1024]{1,0:T(8,128)(2,1)}, bf16[1024,4096]{1,0:T(8,128)(2,1)}) custom-call(s32[8,32]{1,0:T(8,128)} %mask_hbm.1, bf16[32,4096]{1,0:T(8,128)(2,1)S(1)} %get-tuple-element.10.final, bf16[512,1024]{1,0:T(8,128)(2,1)S(1)} %get-tuple-element.11.gate_grad, ...), custom_call_target="tpu_custom_call" | custom-call | tf_op jit(solution)/shard_map/pallas_call | solution.py:631

commit v6 on v5

--- a/solution.py
+++ b/solution.py
@@ -153,11 +153,6 @@
         weight_loads[c] = pltpu.make_async_copy(
             weight_hbm.at[:, cols], weight.at[:, cols], weight_sem.at[c]
         )
-    for copy in loads:
-        copy.start()
-    for c in FORWARD:
-        weight_loads[c].start()
-
     barrier = pltpu.get_barrier_semaphore()
     for peer in (x_peer, y_peer, core_peer, inner_peer):
         pl.semaphore_signal(barrier, inc=1, device_id=peer, device_id_type=pl.DeviceIdType.MESH)
@@ -167,6 +162,11 @@
         pl.semaphore_signal(
             barrier, inc=1, device_id=outer_peer, device_id_type=pl.DeviceIdType.MESH
         )
+
+    for copy in loads:
+        copy.start()
+    for c in FORWARD:
+        weight_loads[c].start()
 
     pl.semaphore_wait(barrier, 4 + mid)
 

time: 69 us -> 69 us (level)
  no operation moved by 1% of the time
where the time goes in v6:
time: 69 us; the launch traced here: 68.8 us
  Pallas kernels  67.9 us (98%)
  between operations  0.86 us (1%)
    pallas_call x1, Pallas kernels, fused(): pl.pallas_call(functools.partial(fused_kernel, scale), out_shape=(pltpu.V...  63.8 us
    pallas_call x1, Pallas kernels, hand_on(): pl.pallas_call(functools.partial(hand_on_kernel, scale), out_shape=tuple(...  4.13 us

profile of v6, /device:TPU:0, one launch (start us, length us, event | category | flops | bytes accessed | tf_op | source)
XLA Modules:
  0.0 68.8 jit_solution(3492348915994635003)
XLA Ops:
  0.6 63.8 %shard_map.84 = (bf16[32,4096]{1,0:T(8,128)(2,1)S(1)}, bf16[512,1024]{1,0:T(8,128)(2,1)S(1)}, bf16[512,1024]{1,0:T(8,128)(2,1)S(1)}, bf16[1024,4096]{1,0:T(8,128...) custom-call(bf16[512,1024]{1,0:T(8,128)(2,1)} %gate_hbm.1, ...), custom_call_target="tpu_custom_call" | custom-call | flops 17179869184 | bytes 41943040 | tf_op jit(solution)/shard_map/pallas_call | solution.py:536
  64.4 4.1 %shard_map.85 = (bf16[32,4096]{1,0:T(8,128)(2,1)}, bf16[512,1024]{1,0:T(8,128)(2,1)}, bf16[512,1024]{1,0:T(8,128)(2,1)}, bf16[1024,4096]{1,0:T(8,128)(2,1)}) custom-call(s32[8,32]{1,0:T(8,128)} %mask_hbm.1, bf16[32,4096]{1,0:T(8,128)(2,1)S(1)} %get-tuple-element.10.final, bf16[512,1024]{1,0:T(8,128)(2,1)S(1)} %get-tuple-element.11.gate_grad, ...), custom_call_target="tpu_custom_call" | custom-call | tf_op jit(solution)/shard_map/pallas_call | solution.py:631
